TPU v7x, 128 devices: a whole 4x4x4 slice. The times are simulated.
128 devices in a mesh: ctx: 8 (over z, y_lo), fsdp: 16 (over y_hi, x, core).
Axes of the slice: x: 4, y: 4 (y_hi: 2, y_lo: 2; y = y_hi * 2 + y_lo), z: 4, core: 2. Of those that a mesh axis runs over, the one named last changes fastest.
Arguments:
- tokens: bfloat16 [2048, 2880], P(('ctx', 'fsdp')), may hold values from -6 to 6
- attn_gain: float32 [2880], replicated, may hold values from 0.1 to 1.9
- query_weight: bfloat16 [2880, 4096], P(None, 'fsdp'), may hold values from -4 to 4
- keyval_weight: bfloat16 [1024, 2880], P('fsdp'), may hold values from -0.109375 to 0.109375
- sink_logits: float32 [64], P('fsdp'), may hold values from 1 to 6
- out_weight: bfloat16 [4096, 2880], P('fsdp'), may hold values from -0.09375 to 0.09375
- mlp_gain: float32 [2880], replicated, may hold values from 0.1 to 1.9
- routes: int32 [2048, 4], P(('ctx', 'fsdp')), may hold values from 0 to 63, all different within a row; in each aligned block of 16 rows (0 to 15, 16 to 31, ...) at most 2 rows name the same one
- gate_fixed: int32 [2048, 4], P(('ctx', 'fsdp')), may hold values from 1 to 65533, as said below
- gate_weight: bfloat16 [64, 1440, 2880], P('fsdp', 'ctx'), may hold values from -0.109375 to 0.109375
- up_weight: bfloat16 [64, 1440, 2880], P('fsdp', 'ctx'), may hold values from -0.109375 to 0.109375
- down_weight: bfloat16 [64, 1440, 2880], P('fsdp', 'ctx'), may hold values from -0.15625 to 0.15625
Outputs:
- layer_out: bfloat16 [2048, 2880], P(('ctx', 'fsdp'))
Inputs may be any that keep to these rules, and one draw needn't show every extreme that they name: `routes`: each row names 4 different experts; within the rows of one device (aligned blocks of 16 rows) no expert is named by more than 2 rows, a bound that some block reaches. `gate_fixed`: the 4 values of each row are positive and add up to 65536.
All inputs are finite; a program needn't handle non-finite values.
Results may differ from a plain program's by a relative error of at most 0.018.
Values may be sent and summed in bfloat16 or wider, within the bound.
A program may use at most 128 MiB of HBM per device.

v0:
```python
import jax
import jax.numpy as jnp
from jax import lax
from jax.sharding import PartitionSpec as P

HEADS = 64
KV_HEADS = 8
HEAD_DIM = 64
WINDOW = 128
TOP = 4


rope_theta = 150000.0
norm_eps = 1e-05
glu_alpha = 1.702
fixed_scale = 65536.0


def from_behind(x, axis, by):
    count = lax.axis_size(axis)
    pairs = [(i, i + by) for i in range(count) if 0 <= i + by < count]
    return lax.ppermute(x, axis, pairs)


def rms_scale(values, gain):
    mean_sq = jnp.mean(values * values, axis=-1, keepdims=True)
    return values * lax.rsqrt(mean_sq + norm_eps) * gain


def rotate(tensor, positions):
    half_dim = tensor.shape[-1] // 2
    freqs = rope_theta ** (-(jnp.arange(half_dim, dtype=jnp.float32) * 2.0 / tensor.shape[-1]))
    angles = positions[:, None] * freqs[None, :]
    cosine = jnp.cos(angles)[:, None, :]
    sine = jnp.sin(angles)[:, None, :]
    first = tensor[..., :half_dim]
    second = tensor[..., half_dim:]
    return jnp.concatenate(
        [first * cosine - second * sine, second * cosine + first * sine], axis=-1
    )


def expert_slots(route_block, num_experts, capacity):
    flat_ids = route_block.reshape(-1)
    onehot = (flat_ids[:, None] == jnp.arange(num_experts, dtype=jnp.int32)[None, :]).astype(
        jnp.int32
    )
    before = jnp.cumsum(onehot, axis=0) - onehot
    slot = jnp.sum(before * onehot, axis=1)
    return flat_ids * capacity + slot


def shards(
    tokens,
    attn_gain,
    query_weight,
    keyval_weight,
    sink_logits,
    out_weight,
    mlp_gain,
    routes,
    gate_fixed,
    gate_weight,
    up_weight,
    down_weight,
):
    ctx_size = lax.axis_size("ctx")
    fsdp_size = lax.axis_size("fsdp")
    ctx_index = lax.axis_index("ctx")
    fsdp_index = lax.axis_index("fsdp")
    local_rows = tokens.shape[0]
    width = tokens.shape[1]
    shard_len = local_rows * fsdp_size
    heads_here = query_weight.shape[1] // HEAD_DIM
    kv_blocks = keyval_weight.shape[0] // HEAD_DIM
    block_ids = fsdp_index * kv_blocks + jnp.arange(kv_blocks, dtype=jnp.int32)
    rope_flag = jnp.concatenate(
        [jnp.ones((heads_here,), jnp.float32), (block_ids < KV_HEADS).astype(jnp.float32)]
    )
    piece = lax.all_gather(tokens, "fsdp", axis=0, tiled=True)
    count = piece.shape[0]
    normed = rms_scale(piece.astype(jnp.float32), attn_gain).astype(jnp.bfloat16)
    query_val = jnp.dot(normed, query_weight, preferred_element_type=jnp.float32)
    kv_val = lax.dot_general(
        normed, keyval_weight, (((1,), (1,)), ((), ())), preferred_element_type=jnp.float32
    )
    mixed = jnp.concatenate([query_val, kv_val], axis=1).reshape(
        count, heads_here + kv_blocks, HEAD_DIM
    )
    positions = (ctx_index * shard_len + jnp.arange(count, dtype=jnp.int32)).astype(jnp.float32)
    turned = rotate(mixed, positions)
    chosen = jnp.where(rope_flag[None, :, None] > 0.5, turned, mixed)
    projected = chosen.astype(jnp.bfloat16).reshape(count, (heads_here + kv_blocks) * HEAD_DIM)
    query_part = projected[:, : heads_here * HEAD_DIM].reshape(shard_len, heads_here, HEAD_DIM)
    kv_mine = projected[:, heads_here * HEAD_DIM :]
    own_head = fsdp_index * heads_here // (HEADS // KV_HEADS)
    kv_all = lax.all_gather(kv_mine, "fsdp", axis=1, tiled=True)
    key_cols = lax.dynamic_slice_in_dim(kv_all, own_head * HEAD_DIM, HEAD_DIM, 1)
    value_cols = lax.dynamic_slice_in_dim(
        kv_all, KV_HEADS * HEAD_DIM + own_head * HEAD_DIM, HEAD_DIM, 1
    )
    own_rows = jnp.concatenate([key_cols, value_cols], axis=1)
    rim_rows = from_behind(own_rows[shard_len - WINDOW :], "ctx", 1)
    extended = jnp.concatenate([rim_rows, own_rows], axis=0)
    key_ext = extended[:, :HEAD_DIM]
    value_ext = extended[:, HEAD_DIM:]
    scores = jnp.einsum(
        "rhd,kd->hrk", query_part, key_ext, preferred_element_type=jnp.float32
    ) * HEAD_DIM ** (-0.5)
    query_pos = ctx_index * shard_len + jnp.arange(shard_len, dtype=jnp.int32)
    key_pos = ctx_index * shard_len - WINDOW + jnp.arange(shard_len + WINDOW, dtype=jnp.int32)
    allowed = (
        (key_pos[None, :] <= query_pos[:, None])
        & (key_pos[None, :] > query_pos[:, None] - WINDOW)
        & (key_pos[None, :] >= 0)
    )
    masked = jnp.where(allowed[None], scores, -1e30)
    top_score = jnp.maximum(jnp.max(masked, axis=-1), sink_logits[:, None])
    expd = jnp.exp(masked - top_score[..., None])
    total = jnp.exp(sink_logits[:, None] - top_score) + jnp.sum(expd, axis=-1)
    probs = (expd / total[..., None]).astype(jnp.bfloat16)
    attended = jnp.einsum("hrk,kd->rhd", probs, value_ext, preferred_element_type=jnp.float32)
    attended = attended.astype(jnp.bfloat16).reshape(shard_len, heads_here * HEAD_DIM)
    attn_delta = lax.psum_scatter(
        jnp.dot(attended, out_weight, preferred_element_type=jnp.float32).astype(jnp.bfloat16),
        "fsdp",
        scatter_dimension=0,
        tiled=True,
    ).astype(jnp.float32)
    resid = tokens.astype(jnp.float32) + attn_delta
    ffn_in = rms_scale(resid, mlp_gain).astype(jnp.bfloat16)
    experts_here = gate_weight.shape[0]
    num_experts = experts_here * fsdp_size
    capacity = max(2, 3 * local_rows * TOP // (2 * num_experts))
    slot_pos = expert_slots(routes, num_experts, capacity)
    table = jnp.any(
        slot_pos.reshape(local_rows, TOP)[None, :, :]
        == jnp.arange(num_experts * capacity, dtype=jnp.int32)[:, None, None],
        axis=-1,
    )
    send_rows = jnp.dot(
        table.astype(jnp.bfloat16), ffn_in, preferred_element_type=jnp.float32
    ).astype(jnp.bfloat16)
    send_rows = send_rows.reshape(fsdp_size, experts_here * capacity, width)
    fanned = jnp.broadcast_to(send_rows[None], (ctx_size,) + send_rows.shape)
    fanned = fanned.reshape(ctx_size * fsdp_size, experts_here * capacity, width)
    arrived = lax.all_to_all(fanned, ("ctx", "fsdp"), split_axis=0, concat_axis=0, tiled=True)
    count = arrived.shape[0]
    grouped = arrived.reshape(count, experts_here, capacity, width)
    gate_val = jnp.einsum(
        "aemd,ehd->aemh", grouped, gate_weight, preferred_element_type=jnp.float32
    )
    up_val = jnp.einsum("aemd,ehd->aemh", grouped, up_weight, preferred_element_type=jnp.float32)
    hidden = (gate_val * jax.nn.sigmoid(glu_alpha * gate_val) * (up_val + 1.0)).astype(jnp.bfloat16)
    partial_value = jnp.einsum(
        "aemh,ehd->aemd", hidden, down_weight, preferred_element_type=jnp.float32
    )
    partial_value = partial_value.reshape(count, experts_here * capacity, width).astype(
        jnp.bfloat16
    )
    returned = lax.all_to_all(
        partial_value, ("ctx", "fsdp"), split_axis=0, concat_axis=0, tiled=True
    )
    returned = returned.reshape(ctx_size, fsdp_size * experts_here * capacity, width).astype(
        jnp.float32
    )
    expert_out = jnp.sum(returned, axis=0).astype(jnp.bfloat16)
    picked = (
        jnp.take(expert_out, slot_pos, axis=0).reshape(local_rows, TOP, width).astype(jnp.float32)
    )
    route_weights = gate_fixed.astype(jnp.float32) / fixed_scale
    moe_sum = jnp.sum(picked * route_weights[..., None], axis=1)
    return (resid + moe_sum).astype(jnp.bfloat16)


def solution(mesh):
    in_specs = (
        P(("ctx", "fsdp"), None),
        P(),
        P(None, "fsdp"),
        P("fsdp", None),
        P("fsdp"),
        P("fsdp", None),
        P(),
        P(("ctx", "fsdp"), None),
        P(("ctx", "fsdp"), None),
        P("fsdp", "ctx", None),
        P("fsdp", "ctx", None),
        P("fsdp", "ctx", None),
    )
    out_specs = P(("ctx", "fsdp"), None)
    return jax.shard_map(shards, mesh=mesh, in_specs=in_specs, out_specs=out_specs, check_vma=False)
```

profile of v0, /device:TPU:1, one launch (start us, length us, event | category | flops | bytes accessed | tf_op | source)
XLA Modules:
  0.0 372.8 jit_solution(805845723172220271)
XLA Ops:
  6.5 0.0 copy-start
  6.5 0.0 all-gather.2.cloned.1.call-start
  6.5 0.7 all-gather.2.cloned.1.call-update
  7.3 0.0 reduce-scatter.2.cloned.1.call-start
  7.3 0.1 fusion.43
  7.4 0.1 broadcast_in_dim.35
  7.5 0.1 broadcast_in_dim.36
  7.6 0.2 multiply_cosine_fusion
  7.8 52.0 %all-gather.2.cloned.1.call-done = bf16[256,2880]{1,0:T(8,128)(2,1)} async-done(((bf16[16,2880]{1,0:T(8,128)(2,1)}), bf16[256,2880]{1,0:T(8,128)(2,1)}) %all-gather.2.cloned.1.call-update) | async-done | bytes 1474576 | tf_op jit(solution)/shard_map/all_gather | solution.py:80
  59.8 1.9 fusion.5
  61.7 2.7 fusion.31
  64.4 0.0 copy-done.9
  64.4 0.0 copy-done.8
  64.5 0.0 copy-done.2
  64.5 0.7 fusion.29
  65.1 0.0 copy-start.6
  65.3 0.1 fusion.36
  65.4 22.8 %all_gather.7 = bf16[256,1024]{0,1:T(8,128)(2,1)S(1)} all-gather(bf16[256,64]{0,1:T(8,128)(2,1)S(1)} %slice.32), channel_id=1, replica_groups=mesh['ctx'=8,'fsdp'=16] {'fsdp'}, dimensions={1}, use_global_device_ids=true | all-gather | bytes 557056 | tf_op jit(solution)/shard_map/all_gather | solution.py:97
  88.2 3.1 collective-permute-start
  91.3 0.2 and_and_fusion
  91.5 0.8 collective-permute-done
  92.3 0.4 fusion.49
  92.8 0.0 copy-done.6
  92.8 0.1 broadcast_maximum_fusion
  92.8 0.2 fusion.8
  93.1 0.1 exponential_add_fusion
  93.1 0.4 convolution_convert_fusion.3
  93.6 0.0 copy-start.5
  93.6 0.0 copy-start.1
  93.6 0.0 copy-start.4
  93.6 0.0 copy-done
  93.6 1.8 convolution_convert_fusion.1
  95.4 0.0 reduce-scatter.2.cloned.1.call-update
  95.4 0.0 copy-done.5
  95.4 0.1 copy.30
  95.5 0.1 reshape.297
  95.6 0.1 fusion.39
  95.7 0.1 reduce_window_sum.11
  95.8 0.2 select_reduce_fusion
  95.9 0.1 reduce_sum.64
  96.1 0.1 copy.32
  96.1 0.1 fusion.40
  96.2 66.4 %reduce-scatter.2.cloned.1.call-done = bf16[16,2880]{1,0:T(8,128)(2,1)} async-done(((bf16[256,2880]{1,0:T(8,128)(2,1)}), bf16[16,2880]{1,0:T(8,128)(2,1)}) %reduce-scatter.2.cloned.1.call-update) | async-done | bytes 92176 | tf_op jit(solution)/shard_map/reduce_scatter | solution.py:124
  162.6 1.0 multiply_reduce_fusion.1
  163.7 0.0 copy-done.4
  163.7 1.4 convolution_convert_fusion.2
  165.1 0.3 copy.33
  165.4 0.8 broadcast_in_dim.70
  166.2 81.2 %all_to_all.10 = bf16[128,8,2880]{2,1,0:T(8,128)(2,1)} all-to-all(bf16[128,8,2880]{2,1,0:T(8,128)(2,1)S(1)} %bitcast.56), channel_id=1, replica_groups=mesh['ctx'=8,'fsdp'=16] {'ctx','fsdp'}, dimensions={0} | all-to-all | bytes 11796480 | tf_op jit(solution)/shard_map/all_to_all | solution.py:147
  247.4 9.0 %copy.34 = bf16[128,8,2880]{0,2,1:T(8,128)(2,1)} copy(bf16[128,8,2880]{2,1,0:T(8,128)(2,1)} %all_to_all.10) | data formatting | bytes 11796480 | tf_op jit(solution)/shard_map/all_to_all | solution.py:147
  256.4 5.3 %fusion.9 = f32[128,4,2,180]{0,3,2,1:T(8,128)S(1)} fusion(bf16[128,4,2,2880]{0,3,2,1:T(8,128)(2,1)} %bitcast.57, bf16[4,180,2880,1]{2,0,1,3:T(4,128)(2,1)} %bitcast.60), kind=kOutput, calls=%fused_computation.19 | convolution fusion | flops 1061683200 | bytes 10782720 | tf_op jit(solution)/shard_map/aemd,ehd->aemh/dot_general | solution.py:150
  261.7 10.7 %convolution_convert_fusion = bf16[4,128,2,2880]{1,3,2,0:T(8,128)(2,1)} fusion(bf16[4,180,2880,1]{2,0,1,3:T(4,128)(2,1)} %bitcast.65, bf16[128,4,2,2880]{0,3,2,1:T(8,128)(2,1)} %bitcast.58, bf16[4,180,2880,1]{2,0,1,3:T(4,128)(2,1)} %bitcast.66, f32[128,4,2,180]{0,3,2,1:T(8,128)S(1)} %fusion.9), kind=kOutput, calls=%fused_computation.2 | convolution fusion | flops 2127790080 | bytes 20828160 | tf_op jit(solution)/shard_map/aemh,ehd->aemd/dot_general | solution.py:155
  272.4 8.8 %copy.38 = bf16[128,8,2880]{2,1,0:T(8,128)(2,1)} copy(bf16[128,8,2880]{0,2,1:T(8,128)(2,1)} %bitcast.59) | data formatting | bytes 11796480 | tf_op jit(solution)/shard_map/convert_element_type | solution.py:158
  281.2 6.0 %all-to-all-start.1 = ((bf16[128,8,2880]{2,1,0:T(8,128)(2,1)}), bf16[128,8,2880]{2,1,0:T(8,128)(2,1)}, u32[]{:S(2)}, u32[]{:S(2)}) async-start(bf16[128,8,2880]{2,1,0:T(8,128)(2,1)} %copy.38), calls=%async_computation.2 | async-start | bytes 12058624 | tf_op jit(solution)/shard_map/all_to_all | solution.py:161
  287.3 0.1 mul.186
  287.3 0.0 copy-done.7
  287.4 0.1 copy.39
  287.5 72.7 %all-to-all-done.1 = bf16[128,8,2880]{2,1,0:T(8,128)(2,1)} async-done(((bf16[128,8,2880]{2,1,0:T(8,128)(2,1)}), bf16[128,8,2880]{2,1,0:T(8,128)(2,1)}, u32[]{:S(2)}, u32[]{:S(2)}) %all-to-all-start.1) | async-done | bytes 5898272 | tf_op jit(solution)/shard_map/all_to_all | solution.py:161
  360.2 3.5 bitcast_reduce_fusion
  363.7 0.0 copy-start.3
  363.7 0.8 gather_fusion
  364.5 0.1 gather.7
  364.6 0.6 multiply_reduce_fusion
  365.3 0.7 add_convert_fusion
  (26 shorter events, 0.2 us)
Async XLA Ops:
  6.5 87.1 %copy-start = (bf16[256,2880]{0,1:T(8,128)(2,1)S(1)}, bf16[256,2880]{0,1:T(8,128)(2,1)}, u32[]{:S(2)}) copy-start(bf16[256,2880]{0,1:T(8,128)(2,1)} %param.17) | copy-start | bytes 4423684
  6.5 57.9 %copy-start.9 = (f32[2880]{0:T(1024)S(1)}, f32[2880]{0:T(1024)}, u32[]{:S(2)}) copy-start(f32[2880]{0:T(1024)} %param.13) | copy-start | bytes 34564
  6.5 57.9 %copy-start.8 = (bf16[64,2880]{1,0:T(8,128)(2,1)S(1)}, bf16[64,2880]{1,0:T(8,128)(2,1)}, u32[]{:S(2)}) copy-start(bf16[64,2880]{1,0:T(8,128)(2,1)} %param.15) | copy-start | bytes 1105924
  6.5 53.3 %all-gather.2.cloned.1.call-start = ((), (), s32[]{:S(2)}) async-start(), calls=%async_computation.3 | async-start | bytes 1601536 | tf_op jit(solution)/shard_map/all_gather | solution.py:80
  7.3 155.4 %reduce-scatter.2.cloned.1.call-start = ((), (), s32[]{:S(2)}) async-start(), calls=%async_computation.4 | async-start | bytes 1601536 | tf_op jit(solution)/shard_map/reduce_scatter | solution.py:124
  59.8 4.6 %copy-start.2 = (bf16[256,2880]{1,0:T(8,128)(2,1)S(1)}, bf16[256,2880]{1,0:T(8,128)(2,1)}, u32[]{:S(2)}) copy-start(bf16[256,2880]{1,0:T(8,128)(2,1)} %all-gather.2.cloned.1.call-done) | copy-start | bytes 4423684
  65.1 27.6 %copy-start.6 = (f32[4]{0:T(128)S(1)}, f32[4]{0:T(128)}, u32[]{:S(2)}) copy-start(f32[4]{0:T(128)} %param.16) | copy-start | bytes 52
  88.2 4.1 %collective-permute-start = (bf16[128,128]{0,1:T(8,128)(2,1)S(1)}, bf16[128,128]{0,1:T(8,128)(2,1)S(1)}, u32[]{:S(2)}, u32[]{:S(2)}) collective-permute-start(bf16[128,128]{0,1:T(8,128)(2,1)S(1)} %pad_maximum_fusion.2), channel_id=1, source_target_pairs={{0,16},{16,32},{32,48},{48,64},{64,80},{80,96},{96,112},{1,17},{17... | collective-permute-start | bytes 98312 | tf_op jit(solution)/shard_map/ppermute | solution.py:22
  93.6 1.8 copy-start.5
  93.6 69.1 %copy-start.1 = (bf16[16,2880]{1,0:T(8,128)(2,1)S(1)}, bf16[16,2880]{1,0:T(8,128)(2,1)}, u32[]{:S(2)}) copy-start(bf16[16,2880]{1,0:T(8,128)(2,1)} %param.12) | copy-start | bytes 276484
  93.6 70.1 %copy-start.4 = (f32[2880]{0:T(1024)S(1)}, f32[2880]{0:T(1024)}, u32[]{:S(2)}) copy-start(f32[2880]{0:T(1024)} %param.18) | copy-start | bytes 34564
  281.2 6.1 %copy-start.7 = (s32[16,4]{0,1:T(4,128)S(1)}, s32[16,4]{0,1:T(4,128)}, u32[]{:S(2)}) copy-start(s32[16,4]{0,1:T(4,128)} %param.20) | copy-start | bytes 772
  281.2 79.0 %all-to-all-start.1 = ((bf16[128,8,2880]{2,1,0:T(8,128)(2,1)}), bf16[128,8,2880]{2,1,0:T(8,128)(2,1)}, u32[]{:S(2)}, u32[]{:S(2)}) async-start(bf16[128,8,2880]{2,1,0:T(8,128)(2,1)} %copy.38), calls=%async_computation.2 | async-start | bytes 12058624 | tf_op jit(solution)/shard_map/all_to_all | solution.py:161
  363.7 1.5 copy-start.3
Sparse Core Ops, SparseCore 0:
  9.7 50.0 all-gather.1
  95.5 67.0 reduce-scatter.1
where the time goes:
time: 374 us; the launch traced here: 373 us
  waiting for transfers between devices  193 us (52%)
  blocking collectives  104 us (28%)
  matrix products  23.4 us (6%)
  local copies, waits for them, and re-layouts  20.5 us (5%)
  between operations  13.8 us (4%)
  other arithmetic  9.33 us (2%)
  starting transfers between devices  9.18 us (2%)
    all_to_all x1, blocking collectives, shards(): lax.all_to_all(fanned, ('ctx', 'fsdp'), split_axis=0, concat_axis=0, tile...  81.2 us
    all_to_all x1, waiting for transfers between devices, shards(): lax.all_to_all(partial_value, ('ctx', 'fsdp'), split_axis=0, concat_axis=...  72.7 us
    reduce_scatter x1, waiting for transfers between devices, shards(): lax.psum_scatter(jnp.dot(attended, out_weight, preferred_element_type=jnp...  66.4 us
    all_gather x1, waiting for transfers between devices, shards(): piece = lax.all_gather(tokens, 'fsdp', axis=0, tiled=True)  52 us
    all_gather x1, blocking collectives, shards(): kv_all = lax.all_gather(kv_mine, 'fsdp', axis=1, tiled=True)  22.8 us
    dot_general x1, matrix products, shards(): jnp.einsum('aemh,ehd->aemd', hidden, down_weight, preferred_element_type=...  10.7 us
    all_to_all x1, local copies, waits for them, and re-layouts, shards(): lax.all_to_all(fanned, ('ctx', 'fsdp'), split_axis=0, concat_axis=0, tile...  8.99 us
    convert_element_type x1, local copies, waits for them, and re-layouts, shards(): partial_value.reshape(count, experts_here * capacity, width)  8.79 us
  transfers between devices with their start and end apart: 4, of which 4 were waited for; matrix products, arithmetic and copies ran while one was open for 0% of the time, Pallas kernels for 0%

commit v1 on v0

--- a/solution.py
+++ b/solution.py
@@ -42,11 +42,9 @@
 
 def expert_slots(route_block, num_experts, capacity):
     flat_ids = route_block.reshape(-1)
-    onehot = (flat_ids[:, None] == jnp.arange(num_experts, dtype=jnp.int32)[None, :]).astype(
-        jnp.int32
-    )
-    before = jnp.cumsum(onehot, axis=0) - onehot
-    slot = jnp.sum(before * onehot, axis=1)
+    order = jnp.arange(flat_ids.shape[0], dtype=jnp.int32)
+    earlier = (order[None, :] < order[:, None]) & (flat_ids[None, :] == flat_ids[:, None])
+    slot = jnp.sum(earlier.astype(jnp.int32), axis=1)
     return flat_ids * capacity + slot
 
 

time: 374 us -> 374 us (level)
  no operation moved by 1% of the time
where the time goes in v1:
time: 374 us; the launch traced here: 373 us
  waiting for transfers between devices  193 us (52%)
  blocking collectives  104 us (28%)
  matrix products  23.4 us (6%)
  local copies, waits for them, and re-layouts  20.5 us (5%)
  between operations  13.8 us (4%)
  starting transfers between devices  9.18 us (2%)
  other arithmetic  9.16 us (2%)
    all_to_all x1, blocking collectives, shards(): lax.all_to_all(fanned, ('ctx', 'fsdp'), split_axis=0, concat_axis=0, tile...  81.2 us
    all_to_all x1, waiting for transfers between devices, shards(): lax.all_to_all(partial_value, ('ctx', 'fsdp'), split_axis=0, concat_axis=...  72.7 us
    reduce_scatter x1, waiting for transfers between devices, shards(): lax.psum_scatter(jnp.dot(attended, out_weight, preferred_element_type=jnp...  66.6 us
    all_gather x1, waiting for transfers between devices, shards(): piece = lax.all_gather(tokens, 'fsdp', axis=0, tiled=True)  52 us
    all_gather x1, blocking collectives, shards(): kv_all = lax.all_gather(kv_mine, 'fsdp', axis=1, tiled=True)  22.8 us
    dot_general x1, matrix products, shards(): jnp.einsum('aemh,ehd->aemd', hidden, down_weight, preferred_element_type=...  10.7 us
    all_to_all x1, local copies, waits for them, and re-layouts, shards(): lax.all_to_all(fanned, ('ctx', 'fsdp'), split_axis=0, concat_axis=0, tile...  8.99 us
    convert_element_type x1, local copies, waits for them, and re-layouts, shards(): partial_value.reshape(count, experts_here * capacity, width)  8.79 us
  transfers between devices with their start and end apart: 4, of which 4 were waited for; matrix products, arithmetic and copies ran while one was open for 0% of the time, Pallas kernels for 0%

profile of v1, /device:TPU:1, one launch (start us, length us, event | category | flops | bytes accessed | tf_op | source)
XLA Modules:
  0.0 372.8 jit_solution(18240761106038815735)
XLA Ops:
  6.5 0.0 copy-start
  6.5 0.0 all-gather.2.cloned.1.call-start
  6.5 0.7 all-gather.2.cloned.1.call-update
  7.3 0.0 reduce-scatter.2.cloned.1.call-start
  7.3 0.1 fusion.43
  7.4 0.1 broadcast_in_dim.35
  7.5 0.1 broadcast_in_dim.36
  7.6 0.2 multiply_cosine_fusion
  7.8 52.0 %all-gather.2.cloned.1.call-done = bf16[256,2880]{1,0:T(8,128)(2,1)} async-done(((bf16[16,2880]{1,0:T(8,128)(2,1)}), bf16[256,2880]{1,0:T(8,128)(2,1)}) %all-gather.2.cloned.1.call-update) | async-done | bytes 1474576 | tf_op jit(solution)/shard_map/all_gather | solution.py:78
  59.8 1.9 fusion.5
  61.7 2.7 fusion.31
  64.4 0.0 copy-done.9
  64.4 0.0 copy-done.8
  64.5 0.0 copy-done.2
  64.5 0.7 fusion.29
  65.1 0.0 copy-start.6
  65.3 0.1 fusion.36
  65.4 22.8 %all_gather.7 = bf16[256,1024]{0,1:T(8,128)(2,1)S(1)} all-gather(bf16[256,64]{0,1:T(8,128)(2,1)S(1)} %slice.32), channel_id=1, replica_groups=mesh['ctx'=8,'fsdp'=16] {'fsdp'}, dimensions={1}, use_global_device_ids=true | all-gather | bytes 557056 | tf_op jit(solution)/shard_map/all_gather | solution.py:95
  88.2 3.1 collective-permute-start
  91.3 0.2 and_and_fusion
  91.5 0.8 collective-permute-done
  92.3 0.4 fusion.49
  92.8 0.0 copy-done.6
  92.8 0.1 broadcast_maximum_fusion
  92.8 0.2 fusion.8
  93.1 0.1 exponential_add_fusion
  93.1 0.4 convolution_convert_fusion.3
  93.6 0.0 copy-start.5
  93.6 0.0 copy-start.1
  93.6 0.0 copy-start.4
  93.6 0.0 copy-done
  93.6 1.8 convolution_convert_fusion.1
  95.4 0.0 reduce-scatter.2.cloned.1.call-update
  95.4 0.0 copy-done.5
  95.4 0.1 copy.30
  95.5 0.1 reshape.298
  95.6 0.2 convert_reduce_fusion
  95.8 0.1 reduce_sum.64
  95.9 0.1 copy.32
  96.0 0.1 fusion.40
  96.1 66.6 %reduce-scatter.2.cloned.1.call-done = bf16[16,2880]{1,0:T(8,128)(2,1)} async-done(((bf16[256,2880]{1,0:T(8,128)(2,1)}), bf16[16,2880]{1,0:T(8,128)(2,1)}) %reduce-scatter.2.cloned.1.call-update) | async-done | bytes 92176 | tf_op jit(solution)/shard_map/reduce_scatter | solution.py:122
  162.6 0.0 copy-done.1
  162.6 1.0 multiply_reduce_fusion.1
  163.7 0.0 copy-done.4
  163.7 1.4 convolution_convert_fusion.2
  165.0 0.3 copy.33
  165.4 0.8 broadcast_in_dim.45
  166.2 81.2 %all_to_all.10 = bf16[128,8,2880]{2,1,0:T(8,128)(2,1)} all-to-all(bf16[128,8,2880]{2,1,0:T(8,128)(2,1)S(1)} %bitcast.56), channel_id=1, replica_groups=mesh['ctx'=8,'fsdp'=16] {'ctx','fsdp'}, dimensions={0} | all-to-all | bytes 11796480 | tf_op jit(solution)/shard_map/all_to_all | solution.py:145
  247.4 9.0 %copy.34 = bf16[128,8,2880]{0,2,1:T(8,128)(2,1)} copy(bf16[128,8,2880]{2,1,0:T(8,128)(2,1)} %all_to_all.10) | data formatting | bytes 11796480 | tf_op jit(solution)/shard_map/all_to_all | solution.py:145
  256.4 5.3 %fusion.9 = f32[128,4,2,180]{0,3,2,1:T(8,128)S(1)} fusion(bf16[128,4,2,2880]{0,3,2,1:T(8,128)(2,1)} %bitcast.57, bf16[4,180,2880,1]{2,0,1,3:T(4,128)(2,1)} %bitcast.60), kind=kOutput, calls=%fused_computation.19 | convolution fusion | flops 1061683200 | bytes 10782720 | tf_op jit(solution)/shard_map/aemd,ehd->aemh/dot_general | solution.py:148
  261.7 10.7 %convolution_convert_fusion = bf16[4,128,2,2880]{1,3,2,0:T(8,128)(2,1)} fusion(bf16[4,180,2880,1]{2,0,1,3:T(4,128)(2,1)} %bitcast.65, bf16[128,4,2,2880]{0,3,2,1:T(8,128)(2,1)} %bitcast.58, bf16[4,180,2880,1]{2,0,1,3:T(4,128)(2,1)} %bitcast.66, f32[128,4,2,180]{0,3,2,1:T(8,128)S(1)} %fusion.9), kind=kOutput, calls=%fused_computation.2 | convolution fusion | flops 2127790080 | bytes 20828160 | tf_op jit(solution)/shard_map/aemh,ehd->aemd/dot_general | solution.py:153
  272.4 8.8 %copy.38 = bf16[128,8,2880]{2,1,0:T(8,128)(2,1)} copy(bf16[128,8,2880]{0,2,1:T(8,128)(2,1)} %bitcast.59) | data formatting | bytes 11796480 | tf_op jit(solution)/shard_map/convert_element_type | solution.py:156
  281.2 6.0 %all-to-all-start.1 = ((bf16[128,8,2880]{2,1,0:T(8,128)(2,1)}), bf16[128,8,2880]{2,1,0:T(8,128)(2,1)}, u32[]{:S(2)}, u32[]{:S(2)}) async-start(bf16[128,8,2880]{2,1,0:T(8,128)(2,1)} %copy.38), calls=%async_computation.2 | async-start | bytes 12058624 | tf_op jit(solution)/shard_map/all_to_all | solution.py:159
  287.3 0.1 mul.182
  287.3 0.0 copy-done.7
  287.4 0.1 copy.39
  287.5 72.7 %all-to-all-done.1 = bf16[128,8,2880]{2,1,0:T(8,128)(2,1)} async-done(((bf16[128,8,2880]{2,1,0:T(8,128)(2,1)}), bf16[128,8,2880]{2,1,0:T(8,128)(2,1)}, u32[]{:S(2)}, u32[]{:S(2)}) %all-to-all-start.1) | async-done | bytes 5898272 | tf_op jit(solution)/shard_map/all_to_all | solution.py:159
  360.2 3.5 bitcast_reduce_fusion
  363.7 0.0 copy-start.3
  363.7 0.8 gather_fusion
  364.5 0.1 gather.7
  364.6 0.6 multiply_reduce_fusion
  365.2 0.0 copy-done.3
  365.2 0.7 add_convert_fusion
  (24 shorter events, 0.2 us)
Async XLA Ops:
  6.5 87.1 %copy-start = (bf16[256,2880]{0,1:T(8,128)(2,1)S(1)}, bf16[256,2880]{0,1:T(8,128)(2,1)}, u32[]{:S(2)}) copy-start(bf16[256,2880]{0,1:T(8,128)(2,1)} %param.17) | copy-start | bytes 4423684
  6.5 57.9 %copy-start.9 = (f32[2880]{0:T(1024)S(1)}, f32[2880]{0:T(1024)}, u32[]{:S(2)}) copy-start(f32[2880]{0:T(1024)} %param.13) | copy-start | bytes 34564
  6.5 57.9 %copy-start.8 = (bf16[64,2880]{1,0:T(8,128)(2,1)S(1)}, bf16[64,2880]{1,0:T(8,128)(2,1)}, u32[]{:S(2)}) copy-start(bf16[64,2880]{1,0:T(8,128)(2,1)} %param.15) | copy-start | bytes 1105924
  6.5 53.3 %all-gather.2.cloned.1.call-start = ((), (), s32[]{:S(2)}) async-start(), calls=%async_computation.3 | async-start | bytes 1601536 | tf_op jit(solution)/shard_map/all_gather | solution.py:78
  7.3 155.3 %reduce-scatter.2.cloned.1.call-start = ((), (), s32[]{:S(2)}) async-start(), calls=%async_computation.4 | async-start | bytes 1601536 | tf_op jit(solution)/shard_map/reduce_scatter | solution.py:122
  59.8 4.6 %copy-start.2 = (bf16[256,2880]{1,0:T(8,128)(2,1)S(1)}, bf16[256,2880]{1,0:T(8,128)(2,1)}, u32[]{:S(2)}) copy-start(bf16[256,2880]{1,0:T(8,128)(2,1)} %all-gather.2.cloned.1.call-done) | copy-start | bytes 4423684
  65.1 27.6 %copy-start.6 = (f32[4]{0:T(128)S(1)}, f32[4]{0:T(128)}, u32[]{:S(2)}) copy-start(f32[4]{0:T(128)} %param.16) | copy-start | bytes 52
  88.2 4.1 %collective-permute-start = (bf16[128,128]{0,1:T(8,128)(2,1)S(1)}, bf16[128,128]{0,1:T(8,128)(2,1)S(1)}, u32[]{:S(2)}, u32[]{:S(2)}) collective-permute-start(bf16[128,128]{0,1:T(8,128)(2,1)S(1)} %pad_maximum_fusion.2), channel_id=1, source_target_pairs={{0,16},{16,32},{32,48},{48,64},{64,80},{80,96},{96,112},{1,17},{17... | collective-permute-start | bytes 98312 | tf_op jit(solution)/shard_map/ppermute | solution.py:22
  93.6 1.8 copy-start.5
  93.6 69.0 %copy-start.1 = (bf16[16,2880]{1,0:T(8,128)(2,1)S(1)}, bf16[16,2880]{1,0:T(8,128)(2,1)}, u32[]{:S(2)}) copy-start(bf16[16,2880]{1,0:T(8,128)(2,1)} %param.12) | copy-start | bytes 276484
  93.6 70.1 %copy-start.4 = (f32[2880]{0:T(1024)S(1)}, f32[2880]{0:T(1024)}, u32[]{:S(2)}) copy-start(f32[2880]{0:T(1024)} %param.18) | copy-start | bytes 34564
  281.2 6.1 %copy-start.7 = (s32[16,4]{0,1:T(4,128)S(1)}, s32[16,4]{0,1:T(4,128)}, u32[]{:S(2)}) copy-start(s32[16,4]{0,1:T(4,128)} %param.20) | copy-start | bytes 772
  281.2 79.0 %all-to-all-start.1 = ((bf16[128,8,2880]{2,1,0:T(8,128)(2,1)}), bf16[128,8,2880]{2,1,0:T(8,128)(2,1)}, u32[]{:S(2)}, u32[]{:S(2)}) async-start(bf16[128,8,2880]{2,1,0:T(8,128)(2,1)} %copy.38), calls=%async_computation.2 | async-start | bytes 12058624 | tf_op jit(solution)/shard_map/all_to_all | solution.py:159
  363.7 1.5 copy-start.3
Sparse Core Ops, SparseCore 0:
  9.7 50.0 all-gather.1
  95.5 67.0 reduce-scatter.1

commit v2 on v1

--- a/solution.py
+++ b/solution.py
@@ -1,7 +1,349 @@
+import functools
 import jax
 import jax.numpy as jnp
 from jax import lax
+from jax.experimental import pallas as pl
+from jax.experimental.pallas import tpu as pltpu
 from jax.sharding import PartitionSpec as P
+
+PARTS = ((0, 1024, 1024), (1024, 1024, 1024), (2048, 832, 896))
+ORDERS = ((0, 1, 2), (1, 2, 0), (2, 0, 1))
+HALF = 512
+GROUPS = 8
+GLU = 1.702
+
+
+def moe_kernel(
+    xin, resid, gate_hbm, up_hbm, down_hbm, out,
+    x0, x1, x2, d0, d1, d2, s0, s1, s2,
+    gate_w, up_w, down_w, table, lower,
+    ra0, ra1, ra2, rb0, rb1, rb2, rc0, rc1, rc2,
+    wsem, ag_send, ag_recv, sib_send, sib_recv,
+    rs_send, rs_recv, sx_send, sx_recv,
+):
+    xs, ds, ss = (x0, x1, x2), (d0, d1, d2), (s0, s1, s2)
+    rbufs = ((ra0, ra1, ra2), (rb0, rb1, rb2), (rc0, rc1, rc2))
+    ctx = lax.axis_index("ctx")
+    fsdp = lax.axis_index("fsdp")
+    core = fsdp % 2
+    me = (ctx // 2, (fsdp // 8) * 2 + ctx % 2, (fsdp // 2) % 4)
+
+    def device(z, y, x, c):
+        return (z * 2 + y % 2, ((y // 2) * 4 + x) * 2 + c)
+
+    def neighbour(axis, by):
+        at = list(me)
+        at[axis] = (at[axis] + by + 4) % 4
+        return device(*at, core)
+
+    sibling = device(*me, 1 - core)
+
+    def copy(src, dst, ss_, rs_, to):
+        return pltpu.make_async_remote_copy(
+            src_ref=src, dst_ref=dst, send_sem=ss_, recv_sem=rs_,
+            device_id=to, device_id_type=pl.DeviceIdType.MESH,
+        )
+
+    weights = [
+        pltpu.make_async_copy(h, v, wsem.at[i])
+        for i, (h, v) in enumerate(((gate_hbm, gate_w), (up_hbm, up_w), (down_hbm, down_w)))
+    ]
+    for w in weights:
+        w.start()
+
+    barrier = pltpu.get_barrier_semaphore()
+    partners = [neighbour(a, b) for a in range(3) for b in (1, -1)] + [sibling]
+    for p in partners:
+        pl.semaphore_signal(barrier, inc=1, device_id=p, device_id_type=pl.DeviceIdType.MESH)
+
+    for p, (lo, n, held) in enumerate(PARTS):
+        xs[p][me[0], me[1], me[2], core] = xin[:, lo : lo + held]
+
+    r = lax.broadcasted_iota(jnp.int32, (256, 256), 0)
+    c = lax.broadcasted_iota(jnp.int32, (256, 256), 1)
+    lower[...] = jnp.where((r // 16 == c // 16) & (c < r), 1.0, 0.0).astype(jnp.bfloat16)
+    pl.semaphore_wait(barrier, len(partners))
+
+    def view(ref, p, stage, by, cols, which=None):
+        axis = ORDERS[p][stage]
+        free = ORDERS[p][:stage]
+        idx = []
+        for a in range(3):
+            if a in free:
+                idx.append(slice(None))
+            elif a == axis:
+                idx.append((me[a] + by + 4) % 4)
+            else:
+                idx.append(me[a])
+        if which is not None:
+            idx.append(which)
+        return ref.at[tuple(idx) + (slice(None), cols)]
+
+    def halves(p):
+        return pl.ds(0, HALF), pl.ds(HALF, PARTS[p][2] - HALF)
+
+    def whole(p):
+        return pl.ds(0, PARTS[p][2])
+
+    pending = []
+    for p in range(3):
+        v = view(xs[p], p, 0, 0, whole(p), core)
+        cp = copy(v, v, sib_send.at[p, 0, 3], sib_recv.at[p, 0, 3], sibling)
+        cp.start()
+        pending.append(cp)
+
+    def ag(p, st, by, half, k, to):
+        v = view(xs[p], p, st, by, halves(p)[half], core)
+        cp = copy(v, v, ag_send.at[p, st, k], ag_recv.at[p, st, k], to)
+        cp.start()
+        pending.append(cp)
+
+    def ag_wait(p, st, by, half, k):
+        v = view(xs[p], p, st, by, halves(p)[half], core)
+        copy(v, v, ag_send.at[p, st, k], ag_recv.at[p, st, k], sibling).wait_recv()
+
+    def forward(p, st, by, k):
+        v = view(xs[p], p, st, by, whole(p), core)
+        cp = copy(v, v, sib_send.at[p, st, k], sib_recv.at[p, st, k], sibling)
+        cp.start()
+        pending.append(cp)
+
+    for st in range(3):
+        for p in range(3):
+            a = ORDERS[p][st]
+            up, dn = neighbour(a, 1), neighbour(a, -1)
+            ag(p, st, 0, 0, 0, up)
+            ag(p, st, 0, 1, 1, dn)
+            ag(p, st, 0, 1, 2, up)
+            ag(p, st, 0, 0, 3, dn)
+        for p in range(3):
+            a = ORDERS[p][st]
+            up, dn = neighbour(a, 1), neighbour(a, -1)
+            ag_wait(p, st, -1, 0, 0)
+            ag(p, st, -1, 0, 4, up)
+            ag_wait(p, st, 1, 1, 1)
+            ag(p, st, 1, 1, 5, dn)
+        for p in range(3):
+            ag_wait(p, st, -1, 1, 2)
+            forward(p, st, -1, 0)
+            ag_wait(p, st, 1, 0, 3)
+            forward(p, st, 1, 1)
+        for p in range(3):
+            ag_wait(p, st, 2, 0, 4)
+            ag_wait(p, st, 2, 1, 5)
+            forward(p, st, 2, 2)
+    for p in range(3):
+        v = view(xs[p], p, 0, 0, whole(p), 1 - core)
+        copy(v, v, sib_send.at[p, 0, 3], sib_recv.at[p, 0, 3], sibling).wait_recv()
+        for st in range(3):
+            for k, by in enumerate((-1, 1, 2)):
+                v = view(xs[p], p, st, by, whole(p), 1 - core)
+                copy(v, v, sib_send.at[p, st, k], sib_recv.at[p, st, k], sibling).wait_recv()
+    for cp in pending:
+        cp.wait_send()
+
+    first_expert = fsdp * 4
+    lane = lax.broadcasted_iota(jnp.int32, (256, 128), 1)
+    row = lax.broadcasted_iota(jnp.int32, (256, 128), 0)
+    lane_expert = (first_expert + lane // 32).astype(jnp.float32)
+    lane_slot = ((lane % 32) // 16).astype(jnp.float32)
+    same_source = row // 16 == lane % 16
+
+    def dispatch(g, _):
+        z, yh = g // 2, g % 2
+
+        def rows(p):
+            return xs[p][z, pl.ds(yh * 2, 2)].reshape(256, PARTS[p][2])
+
+        last = rows(2)
+        ids = last[:, 768:896].astype(jnp.float32)
+        hit = jnp.zeros((256, 128), jnp.float32)
+        for k in range(4):
+            hit = hit + jnp.where(ids[:, 64 + k : 65 + k] == lane_expert, 1.0, 0.0)
+        rank = jnp.dot(lower[...], hit.astype(jnp.bfloat16), preferred_element_type=jnp.float32)
+        t = jnp.where((rank == lane_slot) & same_source, hit, 0.0)
+        table[g] = t.astype(jnp.bfloat16)
+        pick = t.T.astype(jnp.bfloat16)
+        for p in range(3):
+            src = last if p == 2 else rows(p)
+            got = jnp.dot(pick, src, preferred_element_type=jnp.float32).astype(jnp.bfloat16)
+            for e in range(4):
+                ds[p][e, pl.ds(g * 32, 32), :] = got[e * 32 : (e + 1) * 32]
+        return 0
+
+    lax.fori_loop(0, GROUPS, dispatch, 0)
+
+    for w in weights:
+        w.wait()
+
+    def expert(e, _):
+        gate = jnp.zeros((256, 180), jnp.float32)
+        upv = jnp.zeros((256, 180), jnp.float32)
+        for p, (lo, n, held) in enumerate(PARTS):
+            y = ds[p][e, :, 0:n]
+            nt = (((1,), (1,)), ((), ()))
+            gate = gate + lax.dot_general(y, gate_w[e, :, lo : lo + n], nt, preferred_element_type=jnp.float32)
+            upv = upv + lax.dot_general(y, up_w[e, :, lo : lo + n], nt, preferred_element_type=jnp.float32)
+        meta = ds[2][e, :, 768:896].astype(jnp.float32)
+        weight = jnp.zeros((256, 1), jnp.float32)
+        number = (first_expert + e).astype(jnp.float32)
+        for k in range(4):
+            value = meta[:, 68 + k : 69 + k] * 256.0 + meta[:, 72 + k : 73 + k]
+            weight = weight + jnp.where(meta[:, 64 + k : 65 + k] == number, value, 0.0)
+        hidden = gate * jax.nn.sigmoid(GLU * gate) * (upv + 1.0)
+        hidden = (hidden * (weight * (1.0 / 65536.0))).astype(jnp.bfloat16)
+        for p, (lo, n, held) in enumerate(PARTS):
+            ds[p][e, :, 0:n] = jnp.dot(
+                hidden, down_w[e, :, lo : lo + n], preferred_element_type=jnp.float32
+            ).astype(jnp.bfloat16)
+        return 0
+
+    lax.fori_loop(0, 4, expert, 0)
+
+    pending = []
+    for p in range(3):
+        n = PARTS[p][1]
+
+        def combine(g, _, p=p, n=n):
+            z, yh = g // 2, g % 2
+            y = jnp.concatenate([ds[p][e, pl.ds(g * 32, 32), :] for e in range(4)], axis=0)
+            got = jnp.dot(table[g], y, preferred_element_type=jnp.float32).astype(jnp.bfloat16)
+            xs[p][z, pl.ds(yh * 2, 2)] = got.reshape(2, 4, 2, 16, PARTS[p][2])
+            return 0
+
+        lax.fori_loop(0, GROUPS, combine, 0)
+        for k, by in enumerate((2, 1, -1, 0)):
+            cp = copy(
+                view(xs[p], p, 2, by, whole(p), 1 - core), view(ss[p], p, 2, by, whole(p)),
+                sx_send.at[p, k], sx_recv.at[p, k], sibling,
+            )
+            cp.start()
+            pending.append(cp)
+
+    def add(dst, *others):
+        lead = dst.shape[:-2]
+        count = 1
+        for s in lead:
+            count *= s
+
+        def one(i, _):
+            idx = () if not lead else ((i,) if len(lead) == 1 else (i // 4, i % 4))
+            total = dst[idx].astype(jnp.float32)
+            for o in others:
+                total = total + o[idx].astype(jnp.float32)
+            dst[idx] = total.astype(jnp.bfloat16)
+            return 0
+
+        if lead:
+            lax.fori_loop(0, count, one, 0)
+        else:
+            one(0, 0)
+
+    def rs(p, st, k, src, dst, to):
+        cp = copy(src, dst, rs_send.at[p, st, k], rs_recv.at[p, st, k], to)
+        cp.start()
+        pending.append(cp)
+
+    def rs_wait(p, st, k, dst):
+        copy(dst, dst, rs_send.at[p, st, k], rs_recv.at[p, st, k], sibling).wait_recv()
+
+    def sib_wait(p, k, by):
+        v = view(ss[p], p, 2, by, whole(p))
+        copy(v, v, sx_send.at[p, k], sx_recv.at[p, k], sibling).wait_recv()
+
+    for st in (2, 1, 0):
+        for p in range(3):
+            a = ORDERS[p][st]
+            up, dn = neighbour(a, 1), neighbour(a, -1)
+            ha, hb = halves(p)
+            r = rbufs[p][st]
+            if st == 2:
+                sib_wait(p, 0, 2)
+                add(view(xs[p], p, st, 2, whole(p), core), view(ss[p], p, st, 2, whole(p)))
+            rs(p, st, 0, view(xs[p], p, st, 2, ha, core), r.at[2, ..., ha], up)
+            rs(p, st, 1, view(xs[p], p, st, 2, hb, core), r.at[2, ..., hb], dn)
+        for p in range(3):
+            a = ORDERS[p][st]
+            up, dn = neighbour(a, 1), neighbour(a, -1)
+            ha, hb = halves(p)
+            r = rbufs[p][st]
+            if st == 2:
+                sib_wait(p, 1, 1)
+                add(view(xs[p], p, st, 1, whole(p), core), view(ss[p], p, st, 1, whole(p)))
+            rs(p, st, 2, view(xs[p], p, st, 1, hb, core), r.at[0, ..., hb], up)
+            if st == 2:
+                sib_wait(p, 2, -1)
+                add(view(xs[p], p, st, -1, whole(p), core), view(ss[p], p, st, -1, whole(p)))
+            rs(p, st, 3, view(xs[p], p, st, -1, ha, core), r.at[1, ..., ha], dn)
+        for p in range(3):
+            a = ORDERS[p][st]
+            up, dn = neighbour(a, 1), neighbour(a, -1)
+            ha, hb = halves(p)
+            r = rbufs[p][st]
+            rs_wait(p, st, 0, r.at[2, ..., ha])
+            add(view(xs[p], p, st, 1, ha, core), r.at[2, ..., ha])
+            rs(p, st, 4, view(xs[p], p, st, 1, ha, core), r.at[0, ..., ha], up)
+            rs_wait(p, st, 1, r.at[2, ..., hb])
+            add(view(xs[p], p, st, -1, hb, core), r.at[2, ..., hb])
+            rs(p, st, 5, view(xs[p], p, st, -1, hb, core), r.at[1, ..., hb], dn)
+        for p in range(3):
+            ha, hb = halves(p)
+            r = rbufs[p][st]
+            own = view(xs[p], p, st, 0, whole(p), core)
+            others = [r.at[0], r.at[1]]
+            if st == 2:
+                sib_wait(p, 3, 0)
+                others.append(view(ss[p], p, st, 0, whole(p)))
+            rs_wait(p, st, 2, r.at[0, ..., hb])
+            rs_wait(p, st, 3, r.at[1, ..., ha])
+            rs_wait(p, st, 4, r.at[0, ..., ha])
+            rs_wait(p, st, 5, r.at[1, ..., hb])
+            if st:
+                add(own, *others)
+            else:
+                lo, n, held = PARTS[p]
+                total = own[...].astype(jnp.float32) + r[0].astype(jnp.float32) + r[1].astype(jnp.float32)
+                out[:, lo : lo + n] = (resid[:, lo : lo + n] + total[:, :n]).astype(jnp.bfloat16)
+    for cp in pending:
+        cp.wait_send()
+
+
+def moe(xin, resid, gate_weight, up_weight, down_weight):
+    bf = jnp.bfloat16
+    held = [p[2] for p in PARTS]
+    scratch = (
+        [pltpu.VMEM((4, 4, 4, 2, 16, h), bf) for h in held]
+        + [pltpu.VMEM((4, 256, h), bf) for h in held]
+        + [pltpu.VMEM((4, 4, 4, 16, h), bf) for h in held]
+        + [pltpu.VMEM(w.shape, bf) for w in (gate_weight, up_weight, down_weight)]
+        + [pltpu.VMEM((GROUPS, 256, 128), bf), pltpu.VMEM((256, 256), bf)]
+        + [pltpu.VMEM((3,) + (4,) * s + (16, h), bf) for h in held for s in range(3)]
+        + [
+            pltpu.SemaphoreType.DMA((3,)),
+            pltpu.SemaphoreType.DMA((3, 3, 6)),
+            pltpu.SemaphoreType.DMA((3, 3, 6)),
+            pltpu.SemaphoreType.DMA((3, 3, 4)),
+            pltpu.SemaphoreType.DMA((3, 3, 4)),
+            pltpu.SemaphoreType.DMA((3, 3, 6)),
+            pltpu.SemaphoreType.DMA((3, 3, 6)),
+            pltpu.SemaphoreType.DMA((3, 4)),
+            pltpu.SemaphoreType.DMA((3, 4)),
+        ]
+    )
+    vm = pl.BlockSpec(memory_space=pltpu.VMEM)
+    anym = pl.BlockSpec(memory_space=pl.ANY)
+    return pl.pallas_call(
+        moe_kernel,
+        out_shape=jax.ShapeDtypeStruct(resid.shape, bf),
+        in_specs=[vm, vm, anym, anym, anym],
+        out_specs=vm,
+        scratch_shapes=scratch,
+        compiler_params=pltpu.CompilerParams(
+            collective_id=1, has_side_effects=True, vmem_limit_bytes=60 * 1024 * 1024
+        ),
+        name="moe",
+    )(xin, resid, gate_weight, up_weight, down_weight)
+
 
 HEADS = 64
 KV_HEADS = 8
@@ -38,14 +380,6 @@
     return jnp.concatenate(
         [first * cosine - second * sine, second * cosine + first * sine], axis=-1
     )
-
-
-def expert_slots(route_block, num_experts, capacity):
-    flat_ids = route_block.reshape(-1)
-    order = jnp.arange(flat_ids.shape[0], dtype=jnp.int32)
-    earlier = (order[None, :] < order[:, None]) & (flat_ids[None, :] == flat_ids[:, None])
-    slot = jnp.sum(earlier.astype(jnp.int32), axis=1)
-    return flat_ids * capacity + slot
 
 
 def shards(
@@ -127,48 +461,12 @@
     ).astype(jnp.float32)
     resid = tokens.astype(jnp.float32) + attn_delta
     ffn_in = rms_scale(resid, mlp_gain).astype(jnp.bfloat16)
-    experts_here = gate_weight.shape[0]
-    num_experts = experts_here * fsdp_size
-    capacity = max(2, 3 * local_rows * TOP // (2 * num_experts))
-    slot_pos = expert_slots(routes, num_experts, capacity)
-    table = jnp.any(
-        slot_pos.reshape(local_rows, TOP)[None, :, :]
-        == jnp.arange(num_experts * capacity, dtype=jnp.int32)[:, None, None],
-        axis=-1,
-    )
-    send_rows = jnp.dot(
-        table.astype(jnp.bfloat16), ffn_in, preferred_element_type=jnp.float32
-    ).astype(jnp.bfloat16)
-    send_rows = send_rows.reshape(fsdp_size, experts_here * capacity, width)
-    fanned = jnp.broadcast_to(send_rows[None], (ctx_size,) + send_rows.shape)
-    fanned = fanned.reshape(ctx_size * fsdp_size, experts_here * capacity, width)
-    arrived = lax.all_to_all(fanned, ("ctx", "fsdp"), split_axis=0, concat_axis=0, tiled=True)
-    count = arrived.shape[0]
-    grouped = arrived.reshape(count, experts_here, capacity, width)
-    gate_val = jnp.einsum(
-        "aemd,ehd->aemh", grouped, gate_weight, preferred_element_type=jnp.float32
-    )
-    up_val = jnp.einsum("aemd,ehd->aemh", grouped, up_weight, preferred_element_type=jnp.float32)
-    hidden = (gate_val * jax.nn.sigmoid(glu_alpha * gate_val) * (up_val + 1.0)).astype(jnp.bfloat16)
-    partial_value = jnp.einsum(
-        "aemh,ehd->aemd", hidden, down_weight, preferred_element_type=jnp.float32
-    )
-    partial_value = partial_value.reshape(count, experts_here * capacity, width).astype(
-        jnp.bfloat16
-    )
-    returned = lax.all_to_all(
-        partial_value, ("ctx", "fsdp"), split_axis=0, concat_axis=0, tiled=True
-    )
-    returned = returned.reshape(ctx_size, fsdp_size * experts_here * capacity, width).astype(
-        jnp.float32
-    )
-    expert_out = jnp.sum(returned, axis=0).astype(jnp.bfloat16)
-    picked = (
-        jnp.take(expert_out, slot_pos, axis=0).reshape(local_rows, TOP, width).astype(jnp.float32)
-    )
-    route_weights = gate_fixed.astype(jnp.float32) / fixed_scale
-    moe_sum = jnp.sum(picked * route_weights[..., None], axis=1)
-    return (resid + moe_sum).astype(jnp.bfloat16)
+    high = gate_fixed // 256
+    meta = jnp.concatenate([routes, high, gate_fixed - high * 256], axis=1).astype(jnp.bfloat16)
+    xin = jnp.concatenate(
+        [ffn_in, meta, jnp.zeros((local_rows, 2944 - width - meta.shape[1]), jnp.bfloat16)], axis=1
+    )
+    return moe(xin, resid, gate_weight, up_weight, down_weight)
 
 
 def solution(mesh):

time: 374 us -> 275 us (0.74)
  Pallas kernels: 0 us -> 97.5 us
  waiting for transfers between devices: 193 us -> 110 us
  blocking collectives: 104 us -> 22.8 us
  matrix products: 23.4 us -> 5.68 us
  local copies, waits for them, and re-layouts: 20.5 us -> 12.8 us
  starting transfers between devices: 9.18 us -> 3.15 us
    pallas_call x0 -> x1, Pallas kernels: none -> 97.5 us  [moe(): pl.pallas_call(moe_kernel, out_shape=jax.ShapeDtypeStruct(resid.shape, bf...]
    all_to_all x1 -> x0, blocking collectives: 81.2 us -> none  [shards(): lax.all_to_all(fanned, ('ctx', 'fsdp'), split_axis=0, concat_axis=0, tile...]
    all_to_all x1 -> x0, waiting for transfers between devices: 72.7 us -> none  [shards(): lax.all_to_all(partial_value, ('ctx', 'fsdp'), split_axis=0, concat_axis=...]
    dot_general x3 -> x0, matrix products: 17.4 us -> none  [the longest x1 10.7 us: shards(): jnp.einsum('aemh,ehd->aemd', hidden, down_weight, preferred_element_type=...]
    unnamed x21 -> x33, local copies, waits for them, and re-layouts: 0.13 us -> 11.8 us
    reduce_scatter x1, waiting for transfers between devices: 66.6 us -> 56.9 us  [shards(): lax.psum_scatter(jnp.dot(attended, out_weight, preferred_element_type=jnp...]
    convert_element_type x2 -> x0, local copies, waits for them, and re-layouts: 9.14 us -> none  [the longest x1 8.79 us: shards(): partial_value.reshape(count, experts_here * capacity, width)]
    all_to_all x1 -> x0, local copies, waits for them, and re-layouts: 8.99 us -> none  [shards(): lax.all_to_all(fanned, ('ctx', 'fsdp'), split_axis=0, concat_axis=0, tile...]
  transfers between devices with their start and end apart: 4 -> 3, of which waited for: 4 -> 3; matrix products, arithmetic and copies ran while one was open for 0% -> 4% of each run, Pallas kernels for 0% -> 0%
where the time goes in v2:
time: 275 us; the launch traced here: 272 us
  waiting for transfers between devices  110 us (40%)
  Pallas kernels  97.5 us (35%)
  blocking collectives  22.8 us (8%)
  between operations  13.7 us (5%)
  local copies, waits for them, and re-layouts  12.8 us (5%)
  matrix products  5.68 us (2%)
  other arithmetic  5.58 us (2%)
  starting transfers between devices  3.15 us (1%)
    pallas_call x1, Pallas kernels, moe(): pl.pallas_call(moe_kernel, out_shape=jax.ShapeDtypeStruct(resid.shape, bf...  97.5 us
    reduce_scatter x1, waiting for transfers between devices, shards(): lax.psum_scatter(jnp.dot(attended, out_weight, preferred_element_type=jnp...  56.9 us
    all_gather x1, waiting for transfers between devices, shards(): piece = lax.all_gather(tokens, 'fsdp', axis=0, tiled=True)  52 us
    all_gather x1, blocking collectives, shards(): kv_all = lax.all_gather(kv_mine, 'fsdp', axis=1, tiled=True)  22.8 us
    unnamed x33, local copies, waits for them, and re-layouts  11.8 us
  transfers between devices with their start and end apart: 3, of which 3 were waited for; matrix products, arithmetic and copies ran while one was open for 4% of the time, Pallas kernels for 0%

profile of v2, /device:TPU:1, one launch (start us, length us, event | category | flops | bytes accessed | tf_op | source)
XLA Modules:
  0.0 271.6 jit_solution(3535043736727584879)
XLA Ops:
  6.5 0.0 copy-start
  6.5 0.0 copy-start.9
  6.5 0.0 copy-start.8
  6.5 0.0 all-gather.2.cloned.1.call-start
  6.5 0.7 all-gather.2.cloned.1.call-update
  7.3 0.0 reduce-scatter.2.cloned.1.call-start
  7.3 0.1 fusion.14
  7.4 0.1 broadcast_in_dim.22
  7.5 0.1 broadcast_in_dim.23
  7.6 0.2 multiply_cosine_fusion
  7.8 52.0 %all-gather.2.cloned.1.call-done = bf16[256,2880]{1,0:T(8,128)(2,1)} async-done(((bf16[16,2880]{1,0:T(8,128)(2,1)}), bf16[256,2880]{1,0:T(8,128)(2,1)}) %all-gather.2.cloned.1.call-update) | async-done | bytes 1474576 | tf_op jit(solution)/shard_map/all_gather | solution.py:412
  59.8 1.8 fusion
  61.6 0.0 copy-start.1
  61.6 0.0 copy-start.7
  61.6 0.0 copy-done.9
  61.6 0.0 copy-done.8
  61.6 2.2 fusion.4
  63.9 0.0 copy-done.1
  63.9 0.0 copy-done.7
  63.9 0.9 fusion.6
  64.9 0.1 fusion.8
  65.0 0.0 copy-start.5
  65.0 22.8 %all_gather.7 = bf16[256,1024]{0,1:T(8,128)(2,1)S(1)} all-gather(bf16[256,64]{0,1:T(8,128)(2,1)S(1)} %slice.30), channel_id=1, replica_groups=mesh['ctx'=8,'fsdp'=16] {'fsdp'}, dimensions={1}, use_global_device_ids=true | all-gather | bytes 557056 | tf_op jit(solution)/shard_map/all_gather | solution.py:429
  87.8 3.1 %collective-permute-start = (bf16[128,128]{0,1:T(8,128)(2,1)S(1)}, bf16[128,128]{0,1:T(8,128)(2,1)S(1)}, u32[]{:S(2)}, u32[]{:S(2)}) collective-permute-start(bf16[128,128]{0,1:T(8,128)(2,1)S(1)} %pad_maximum_fusion.2), channel_id=1, source_target_pairs={{0,16},{16,32},{32,48},{48,64},{64,80},{80,96},{96,112},{1,17},{17... | collective-permute-start | bytes 98312 | tf_op jit(solution)/shard_map/ppermute | solution.py:364
  90.9 0.2 and_and_fusion
  91.1 0.8 collective-permute-done
  92.0 0.4 fusion.15
  92.4 0.0 copy-done.5
  92.4 0.1 broadcast_maximum_fusion
  92.5 0.2 fusion.3
  92.7 0.1 exponential_add_fusion
  92.8 0.4 convolution_convert_fusion.1
  93.2 0.0 copy-done
  93.2 0.0 copy-start.6
  93.2 0.0 copy-start.4
  93.2 1.8 convolution_convert_fusion
  95.0 0.0 slice-start
  95.0 0.0 reduce-scatter.2.cloned.1.call-update
  95.0 0.0 copy-done.6
  95.0 0.1 copy.29
  95.1 0.0 copy-done.4
  95.1 0.1 copy.24
  95.2 0.0 slice-start.1
  95.2 0.0 slice-start.2
  95.2 5.0 %copy.30.gate_hbm = bf16[4,180,2880]{2,1,0:T(8,128)(2,1)} copy(bf16[4,180,2880]{2,0,1:T(4,128)(2,1)} %param.21) | data formatting | bytes 8294400 | tf_op args[9]
  100.3 0.0 slice-done
  100.3 0.0 slice-done.1
  100.3 0.0 slice-start.3
  100.3 2.5 copy.31.up_hbm
  102.8 0.0 slice-done.2
  102.8 0.0 slice-done.3
  102.8 0.0 copy-start.2
  102.8 0.0 copy-start.3
  102.8 2.5 copy.32.down_hbm
  105.4 56.9 %reduce-scatter.2.cloned.1.call-done = bf16[16,2880]{1,0:T(8,128)(2,1)} async-done(((bf16[256,2880]{1,0:T(8,128)(2,1)}), bf16[16,2880]{1,0:T(8,128)(2,1)}) %reduce-scatter.2.cloned.1.call-update) | async-done | bytes 92176 | tf_op jit(solution)/shard_map/reduce_scatter | solution.py:456
  162.2 0.0 copy-done.2
  162.2 1.7 convert_add_fusion
  163.9 0.0 copy-done.3
  164.0 1.0 multiply_convert_fusion
  164.9 0.7 concatenate.32.xin
  165.7 97.5 %moe.1 = bf16[16,2880]{1,0:T(8,128)(2,1)} custom-call(bf16[16,2944]{1,0:T(8,128)(2,1)} %concatenate.32.xin, f32[16,2880]{1,0:T(8,128)} %get-tuple-element.9.resid, bf16[4,180,2880]{2,1,0:T(8,128)(2,1)} %copy.30.gate_hbm, bf16[4,180,2880]{2,1,0:T(8,128)(2,1)} %copy.31.up_hbm, bf16[4,180,2880]{2,1,0:T(8,128)(2,1)} %copy.32.down_hbm), custom_call_target="tpu_custom_call" | custom-call | tf_op jit(solution)/shard_map/moe/pallas_call | solution.py:335
  263.2 1.5 copy.35
  (20 shorter events, 0.2 us)
Async XLA Ops:
  6.5 86.7 %copy-start = (bf16[256,2880]{0,1:T(8,128)(2,1)S(1)}, bf16[256,2880]{0,1:T(8,128)(2,1)}, u32[]{:S(2)}) copy-start(bf16[256,2880]{0,1:T(8,128)(2,1)} %param.17) | copy-start | bytes 4423684
  6.5 55.1 %copy-start.9 = (f32[2880]{0:T(1024)S(1)}, f32[2880]{0:T(1024)}, u32[]{:S(2)}) copy-start(f32[2880]{0:T(1024)} %param.13) | copy-start | bytes 34564
  6.5 55.1 %copy-start.8 = (bf16[64,2880]{1,0:T(8,128)(2,1)S(1)}, bf16[64,2880]{1,0:T(8,128)(2,1)}, u32[]{:S(2)}) copy-start(bf16[64,2880]{1,0:T(8,128)(2,1)} %param.15) | copy-start | bytes 1105924
  6.5 53.3 %all-gather.2.cloned.1.call-start = ((), (), s32[]{:S(2)}) async-start(), calls=%async_computation.1 | async-start | bytes 1601536 | tf_op jit(solution)/shard_map/all_gather | solution.py:412
  7.3 155.0 %reduce-scatter.2.cloned.1.call-start = ((), (), s32[]{:S(2)}) async-start(), calls=%async_computation.2 | async-start | bytes 1601536 | tf_op jit(solution)/shard_map/reduce_scatter | solution.py:456
  61.6 2.3 copy-start.1
  61.6 2.3 copy-start.7
  65.0 27.4 %copy-start.5 = (f32[4]{0:T(128)S(1)}, f32[4]{0:T(128)}, u32[]{:S(2)}) copy-start(f32[4]{0:T(128)} %param.16) | copy-start | bytes 52
  87.8 4.1 %collective-permute-start = (bf16[128,128]{0,1:T(8,128)(2,1)S(1)}, bf16[128,128]{0,1:T(8,128)(2,1)S(1)}, u32[]{:S(2)}, u32[]{:S(2)}) collective-permute-start(bf16[128,128]{0,1:T(8,128)(2,1)S(1)} %pad_maximum_fusion.2), channel_id=1, source_target_pairs={{0,16},{16,32},{32,48},{48,64},{64,80},{80,96},{96,112},{1,17},{17... | collective-permute-start | bytes 98312 | tf_op jit(solution)/shard_map/ppermute | solution.py:364
  93.2 1.8 copy-start.6
  93.2 1.9 copy-start.4
  95.0 5.3 %slice-start = ((s8[4239360]{0:T(1024)(128)(4,1)}), s8[45056]{0:T(1024)(128)(4,1)S(1)}, s32[]{:S(2)}) async-start(s8[4239360]{0:T(1024)(128)(4,1)} %bitcast.25), calls=%async_computation.3 | async-start | bytes 90112
  95.2 5.0 %slice-start.1 = ((s8[4239360]{0:T(1024)(128)(4,1)}), s8[4194304]{0:T(1024)(128)(4,1)S(1)}, s32[]{:S(2)}) async-start(s8[4239360]{0:T(1024)(128)(4,1)} %bitcast.25), calls=%async_computation.4 | async-start | bytes 8388608
  95.2 7.6 %slice-start.2 = ((s8[4239360]{0:T(1024)(128)(4,1)}), s8[4194304]{0:T(1024)(128)(4,1)S(1)}, s32[]{:S(2)}) async-start(s8[4239360]{0:T(1024)(128)(4,1)} %bitcast.27), calls=%async_computation.5 | async-start | bytes 8388608
  100.3 2.5 slice-start.3
  102.8 59.4 %copy-start.2 = (bf16[16,2880]{1,0:T(8,128)(2,1)S(1)}, bf16[16,2880]{1,0:T(8,128)(2,1)}, u32[]{:S(2)}) copy-start(bf16[16,2880]{1,0:T(8,128)(2,1)} %param.12) | copy-start | bytes 276484
  102.8 61.1 %copy-start.3 = (f32[2880]{0:T(1024)S(1)}, f32[2880]{0:T(1024)}, u32[]{:S(2)}) copy-start(f32[2880]{0:T(1024)} %param.18) | copy-start | bytes 34564
Sparse Core Ops, SparseCore 0:
  9.7 50.0 all-gather.1
  95.1 67.0 reduce-scatter.1

commit v3 on v2

--- a/solution.py
+++ b/solution.py
@@ -13,13 +13,17 @@
 GLU = 1.702
 
 
-def moe_kernel(
-    xin, resid, gate_hbm, up_hbm, down_hbm, out,
+def layer_kernel(
+    tokens, attn_gain, mlp_gain, cos_ref, sin_ref, sinks, meta,
+    query_hbm, keyval_hbm, outw_hbm, gate_hbm, up_hbm, down_hbm, out,
     x0, x1, x2, d0, d1, d2, s0, s1, s2,
     gate_w, up_w, down_w, table, lower,
     ra0, ra1, ra2, rb0, rb1, rb2, rc0, rc1, rc2,
+    query_w, keyval_w, outw_w, gathered, normed, kv_mine, kv_all, queries, attended,
+    part, part_sib, part_in, part_last, resid,
     wsem, ag_send, ag_recv, sib_send, sib_recv,
     rs_send, rs_recv, sx_send, sx_recv,
+    ta_send, ta_recv, kv_send, kv_recv, tr_send, tr_recv,
 ):
     xs, ds, ss = (x0, x1, x2), (d0, d1, d2), (s0, s1, s2)
     rbufs = ((ra0, ra1, ra2), (rb0, rb1, rb2), (rc0, rc1, rc2))
@@ -44,25 +48,257 @@
             device_id=to, device_id_type=pl.DeviceIdType.MESH,
         )
 
-    weights = [
+    loads = [
         pltpu.make_async_copy(h, v, wsem.at[i])
-        for i, (h, v) in enumerate(((gate_hbm, gate_w), (up_hbm, up_w), (down_hbm, down_w)))
+        for i, (h, v) in enumerate(
+            (
+                (keyval_hbm, keyval_w), (query_hbm, query_w), (outw_hbm, outw_w),
+                (gate_hbm, gate_w), (up_hbm, up_w), (down_hbm, down_w),
+            )
+        )
     ]
-    for w in weights:
+    for w in loads:
         w.start()
+    weights = loads[3:]
+
+    def signal(to):
+        pl.semaphore_signal(barrier, inc=1, device_id=to, device_id_type=pl.DeviceIdType.MESH)
 
     barrier = pltpu.get_barrier_semaphore()
-    partners = [neighbour(a, b) for a in range(3) for b in (1, -1)] + [sibling]
-    for p in partners:
-        pl.semaphore_signal(barrier, inc=1, device_id=p, device_id_type=pl.DeviceIdType.MESH)
-
-    for p, (lo, n, held) in enumerate(PARTS):
-        xs[p][me[0], me[1], me[2], core] = xin[:, lo : lo + held]
-
+    across = device(me[0], (me[1] + 2) % 4, me[2], core)
+    partners = [neighbour(a, b) for a in range(3) for b in (1, -1)] + [sibling, across]
+    for to in partners:
+        signal(to)
+    behind = (ctx + 7) % 8
+    ahead = (ctx + 1) % 8
+    key_from, value_from = fsdp // 2, 8 + fsdp // 2
+    signal((behind, key_from))
+    signal((behind, value_from))
+
+    @pl.when(fsdp != 0)
+    def _():
+        signal((ctx, key_from))
+
+    @pl.when(fsdp != 15)
+    def _():
+        signal((ctx, value_from))
+
+    yh = me[1] // 2
+    gathered[yh, me[2], core] = tokens[...]
     r = lax.broadcasted_iota(jnp.int32, (256, 256), 0)
     c = lax.broadcasted_iota(jnp.int32, (256, 256), 1)
     lower[...] = jnp.where((r // 16 == c // 16) & (c < r), 1.0, 0.0).astype(jnp.bfloat16)
-    pl.semaphore_wait(barrier, len(partners))
+    alone = jnp.where((fsdp == 0) | (fsdp == 15), 1, 0)
+    pl.semaphore_wait(barrier, len(partners) + 4 - alone)
+
+    started = []
+
+    def send(src, dst, send_sem, recv_sem, to):
+        cp = copy(src, dst, send_sem, recv_sem, to)
+        cp.start()
+        started.append(cp)
+
+    left, right = neighbour(2, -1), neighbour(2, 1)
+    halves_of = (pl.ds(0, 1408), pl.ds(1408, 1472))
+
+    def held(b, by, which, half=None):
+        at = gathered.at[(yh + b) % 2, (me[2] + by + 4) % 4, which]
+        return at if half is None else at.at[:, halves_of[half]]
+
+    def pass_on(b, by, half, k, to):
+        v = held(b, by, core, half)
+        send(v, v, ta_send.at[b, k], ta_recv.at[b, k], to)
+
+    def arrived(b, by, half, k):
+        v = held(b, by, core, half)
+        copy(v, v, ta_send.at[b, k], ta_recv.at[b, k], sibling).wait_recv()
+
+    def to_sibling(b, by, k):
+        v = held(b, by, core)
+        send(v, v, ta_send.at[b, k], ta_recv.at[b, k], sibling)
+
+    def norm_block(b, by, which):
+        y_, x_ = (yh + b) % 2, (me[2] + by + 4) % 4
+        v = gathered[y_, x_, which].astype(jnp.float32)
+        scale = lax.rsqrt(jnp.sum(v * v, axis=-1, keepdims=True) * (1.0 / 2880.0) + 1e-05)
+        row = ((y_ * 4 + x_) * 2 + which) * 16
+        normed[pl.ds(pl.multiple_of(row, 16), 16), :] = (v * scale * attn_gain[...]).astype(jnp.bfloat16)
+
+    send(held(0, 0, core), held(0, 0, core), ta_send.at[0, 10], ta_recv.at[0, 10], across)
+    for b in range(2):
+        if b == 1:
+            v = held(1, 0, core)
+            copy(v, v, ta_send.at[0, 10], ta_recv.at[0, 10], sibling).wait_recv()
+        pass_on(b, 0, 0, 0, right)
+        pass_on(b, 0, 1, 1, left)
+        pass_on(b, 0, 1, 2, right)
+        pass_on(b, 0, 0, 3, left)
+        to_sibling(b, 0, 6)
+        norm_block(b, 0, core)
+    for b in range(2):
+        arrived(b, -1, 0, 0)
+        pass_on(b, -1, 0, 4, right)
+        arrived(b, 1, 1, 1)
+        pass_on(b, 1, 1, 5, left)
+    for b in range(2):
+        arrived(b, -1, 1, 2)
+        to_sibling(b, -1, 7)
+        arrived(b, 1, 0, 3)
+        to_sibling(b, 1, 8)
+        norm_block(b, -1, core)
+        norm_block(b, 1, core)
+    for b in range(2):
+        arrived(b, 2, 0, 4)
+        arrived(b, 2, 1, 5)
+        to_sibling(b, 2, 9)
+        norm_block(b, 2, core)
+    for k, by in ((6, 0), (7, -1), (8, 1), (9, 2)):
+        for b in range(2):
+            v = held(b, by, 1 - core)
+            copy(v, v, ta_send.at[b, k], ta_recv.at[b, k], sibling).wait_recv()
+            norm_block(b, by, 1 - core)
+
+    nt = (((1,), (1,)), ((), ()))
+    cosine, sine = cos_ref[...], sin_ref[...]
+    early = lax.broadcasted_iota(jnp.int32, (256, 128), 1) % 64 < 32
+
+    def turn(v, c_, s_):
+        return v * c_ + jnp.where(early, pltpu.roll(v, 96, 1), pltpu.roll(v, 32, 1)) * s_
+
+    loads[0].wait()
+    kv = lax.dot_general(normed[...], keyval_w[...], nt, preferred_element_type=jnp.float32)
+    kv = jnp.concatenate([kv, kv], axis=1)
+    kv = jnp.where(fsdp < 8, turn(kv, cosine, sine), kv)
+    kv_mine[...] = kv[:, :64].astype(jnp.bfloat16)
+    which = fsdp // 8
+    main, rim = pl.ds(128, 256), pl.ds(0, 128)
+    wait_main = []
+    for i in range(2):
+        to = 2 * (fsdp % 8) + i
+        cp = copy(kv_mine, kv_all.at[which, main], kv_send.at[i], kv_recv.at[which * 2], (ctx, to))
+        own = fsdp == 15 * i
+
+        @pl.when(jnp.logical_not(own))
+        def _(cp=cp):
+            cp.start()
+
+        @pl.when(own)
+        def _():
+            kv_all[which, main] = kv_mine[...]
+
+        wait_main.append((own, cp))
+        send(
+            kv_mine.at[pl.ds(128, 128)], kv_all.at[which, rim],
+            kv_send.at[2 + i], kv_recv.at[which * 2 + 1], (ahead, to),
+        )
+    loads[1].wait()
+    query = jnp.dot(normed[...], query_w[...], preferred_element_type=jnp.float32)
+    for i in range(2):
+        cols = slice(i * 128, i * 128 + 128)
+        queries[:, cols] = turn(query[:, cols], cosine, sine).astype(jnp.bfloat16)
+    for w in range(2):
+        v = kv_all.at[w, main]
+
+        @pl.when(fsdp != 15 * w)
+        def _(v=v, w=w):
+            copy(v, v, kv_send.at[0], kv_recv.at[w * 2], sibling).wait_recv()
+
+        v = kv_all.at[w, rim]
+        copy(v, v, kv_send.at[0], kv_recv.at[w * 2 + 1], sibling).wait_recv()
+    for own, cp in wait_main:
+
+        @pl.when(jnp.logical_not(own))
+        def _(cp=cp):
+            cp.wait_send()
+
+    row = lax.broadcasted_iota(jnp.int32, (128, 256), 0)
+    col = lax.broadcasted_iota(jnp.int32, (128, 256), 1)
+    for b in range(2):
+        allowed = (col <= row + 128) & (col > row) & (ctx * 256 + b * 128 - 128 + col >= 0)
+        keys = kv_all[0, b * 128 : b * 128 + 256]
+        values = kv_all[1, b * 128 : b * 128 + 256]
+        for h in range(4):
+            q = queries[b * 128 : b * 128 + 128, h * 64 : h * 64 + 64]
+            score = lax.dot_general(q, keys, nt, preferred_element_type=jnp.float32) * 0.125
+            score = jnp.where(allowed, score, -1e30)
+            sink = sinks[h]
+            top = jnp.maximum(jnp.max(score, axis=-1, keepdims=True), sink)
+            expd = jnp.exp(score - top)
+            total = jnp.exp(sink - top) + jnp.sum(expd, axis=-1, keepdims=True)
+            probs = (expd / total).astype(jnp.bfloat16)
+            mixed = jnp.dot(probs, values, preferred_element_type=jnp.float32)
+            attended[b * 128 : b * 128 + 128, h * 64 : h * 64 + 64] = mixed.astype(jnp.bfloat16)
+
+    loads[2].wait()
+    for lo, n in ((0, 1024), (1024, 1024), (2048, 832)):
+        got = lax.dot_general(
+            attended[...], outw_w[lo : lo + n, :], nt, preferred_element_type=jnp.float32
+        ).astype(jnp.bfloat16)
+        part[:, :, :, :, lo : lo + n] = got.reshape(2, 4, 2, 16, n)
+
+    def piece(by, half=None):
+        cols = slice(None) if half is None else halves_of[half]
+        return part.at[:, (me[2] + by + 4) % 4, core, :, cols]
+
+    def landed(slot, half):
+        return part_in.at[slot, :, :, halves_of[half]]
+
+    def from_sibling(by):
+        return part_sib.at[:, (me[2] + by + 4) % 4]
+
+    def tr_wait(k, v):
+        copy(v, v, tr_send.at[k], tr_recv.at[k], sibling).wait_recv()
+
+    def plus(dst, *others):
+        for i in range(2):
+            total = dst[i].astype(jnp.float32)
+            for o in others:
+                total = total + o[i].astype(jnp.float32)
+            dst[i] = total.astype(jnp.bfloat16)
+
+    for k, by in enumerate((2, 1, -1, 0)):
+        send(
+            part.at[:, (me[2] + by + 4) % 4, 1 - core], from_sibling(by),
+            tr_send.at[k], tr_recv.at[k], sibling,
+        )
+    tr_wait(0, from_sibling(2))
+    plus(piece(2), from_sibling(2))
+    send(piece(2, 0), landed(2, 0), tr_send.at[4], tr_recv.at[4], right)
+    send(piece(2, 1), landed(2, 1), tr_send.at[5], tr_recv.at[5], left)
+    tr_wait(1, from_sibling(1))
+    plus(piece(1), from_sibling(1))
+    send(piece(1, 1), landed(0, 1), tr_send.at[6], tr_recv.at[6], right)
+    tr_wait(2, from_sibling(-1))
+    plus(piece(-1), from_sibling(-1))
+    send(piece(-1, 0), landed(1, 0), tr_send.at[7], tr_recv.at[7], left)
+    tr_wait(4, landed(2, 0))
+    plus(piece(1, 0), landed(2, 0))
+    send(piece(1, 0), landed(0, 0), tr_send.at[8], tr_recv.at[8], right)
+    tr_wait(5, landed(2, 1))
+    plus(piece(-1, 1), landed(2, 1))
+    send(piece(-1, 1), landed(1, 1), tr_send.at[9], tr_recv.at[9], left)
+    tr_wait(3, from_sibling(0))
+    plus(piece(0), from_sibling(0))
+    tr_wait(6, landed(0, 1))
+    tr_wait(7, landed(1, 0))
+    tr_wait(8, landed(0, 0))
+    tr_wait(9, landed(1, 1))
+    plus(piece(0), part_in.at[0], part_in.at[1])
+    send(part.at[1 - yh, me[2], core], part_last, tr_send.at[10], tr_recv.at[10], across)
+    tr_wait(10, part_last)
+    total = part[yh, me[2], core].astype(jnp.float32) + part_last[...].astype(jnp.float32)
+    resid[:, 2816:2944] = jnp.zeros((16, 128), jnp.float32)
+    resid[:, 0:2880] = tokens[...].astype(jnp.float32) + total
+    v = resid[...]
+    scale = lax.rsqrt(jnp.sum(v * v, axis=-1, keepdims=True) * (1.0 / 2880.0) + 1e-05)
+    v = v * scale * mlp_gain[...]
+    for p, (lo, n, wide) in enumerate(PARTS):
+        w = v[:, lo : lo + wide]
+        if p == 2:
+            w = jnp.concatenate([w[:, :768], w[:, 768:] + meta[...]], axis=1)
+        xs[p][me[0], me[1], me[2], core] = w.astype(jnp.bfloat16)
+    for cp in started:
+        cp.wait_send()
 
     def view(ref, p, stage, by, cols, which=None):
         axis = ORDERS[p][stage]
@@ -308,165 +544,79 @@
         cp.wait_send()
 
 
-def moe(xin, resid, gate_weight, up_weight, down_weight):
+def layer(tokens, attn_gain, mlp_gain, cosine, sine, sinks, meta, weights):
     bf = jnp.bfloat16
-    held = [p[2] for p in PARTS]
+    wide = [p[2] for p in PARTS]
+    width = tokens.shape[1]
+    dma = pltpu.SemaphoreType.DMA
     scratch = (
-        [pltpu.VMEM((4, 4, 4, 2, 16, h), bf) for h in held]
-        + [pltpu.VMEM((4, 256, h), bf) for h in held]
-        + [pltpu.VMEM((4, 4, 4, 16, h), bf) for h in held]
-        + [pltpu.VMEM(w.shape, bf) for w in (gate_weight, up_weight, down_weight)]
+        [pltpu.VMEM((4, 4, 4, 2, 16, h), bf) for h in wide]
+        + [pltpu.VMEM((4, 256, h), bf) for h in wide]
+        + [pltpu.VMEM((4, 4, 4, 16, h), bf) for h in wide]
+        + [pltpu.VMEM(w.shape, bf) for w in weights[3:]]
         + [pltpu.VMEM((GROUPS, 256, 128), bf), pltpu.VMEM((256, 256), bf)]
-        + [pltpu.VMEM((3,) + (4,) * s + (16, h), bf) for h in held for s in range(3)]
+        + [pltpu.VMEM((3,) + (4,) * s + (16, h), bf) for h in wide for s in range(3)]
+        + [pltpu.VMEM(w.shape, bf) for w in (weights[0], weights[1], weights[2])]
         + [
-            pltpu.SemaphoreType.DMA((3,)),
-            pltpu.SemaphoreType.DMA((3, 3, 6)),
-            pltpu.SemaphoreType.DMA((3, 3, 6)),
-            pltpu.SemaphoreType.DMA((3, 3, 4)),
-            pltpu.SemaphoreType.DMA((3, 3, 4)),
-            pltpu.SemaphoreType.DMA((3, 3, 6)),
-            pltpu.SemaphoreType.DMA((3, 3, 6)),
-            pltpu.SemaphoreType.DMA((3, 4)),
-            pltpu.SemaphoreType.DMA((3, 4)),
+            pltpu.VMEM((2, 4, 2, 16, width), bf),
+            pltpu.VMEM((256, width), bf),
+            pltpu.VMEM((256, 64), bf),
+            pltpu.VMEM((2, 384, 64), bf),
+            pltpu.VMEM((256, 256), bf),
+            pltpu.VMEM((256, 256), bf),
+            pltpu.VMEM((2, 4, 2, 16, width), bf),
+            pltpu.VMEM((2, 4, 16, width), bf),
+            pltpu.VMEM((3, 2, 16, width), bf),
+            pltpu.VMEM((16, width), bf),
+            pltpu.VMEM((16, 2944), jnp.float32),
+        ]
+        + [
+            dma((6,)), dma((3, 3, 6)), dma((3, 3, 6)), dma((3, 3, 4)), dma((3, 3, 4)),
+            dma((3, 3, 6)), dma((3, 3, 6)), dma((3, 4)), dma((3, 4)),
+            dma((2, 11)), dma((2, 11)), dma((4,)), dma((4,)), dma((11,)), dma((11,)),
         ]
     )
     vm = pl.BlockSpec(memory_space=pltpu.VMEM)
+    sm = pl.BlockSpec(memory_space=pltpu.SMEM)
     anym = pl.BlockSpec(memory_space=pl.ANY)
     return pl.pallas_call(
-        moe_kernel,
-        out_shape=jax.ShapeDtypeStruct(resid.shape, bf),
-        in_specs=[vm, vm, anym, anym, anym],
+        layer_kernel,
+        out_shape=jax.ShapeDtypeStruct(tokens.shape, bf),
+        in_specs=[vm] * 5 + [sm, vm] + [anym] * 6,
         out_specs=vm,
         scratch_shapes=scratch,
         compiler_params=pltpu.CompilerParams(
-            collective_id=1, has_side_effects=True, vmem_limit_bytes=60 * 1024 * 1024
+            collective_id=1, has_side_effects=True, vmem_limit_bytes=62 * 1024 * 1024
         ),
-        name="moe",
-    )(xin, resid, gate_weight, up_weight, down_weight)
-
-
-HEADS = 64
-KV_HEADS = 8
+        name="layer",
+    )(tokens, attn_gain, mlp_gain, cosine, sine, sinks, meta, *weights)
+
+
 HEAD_DIM = 64
-WINDOW = 128
-TOP = 4
-
-
 rope_theta = 150000.0
-norm_eps = 1e-05
-glu_alpha = 1.702
-fixed_scale = 65536.0
-
-
-def from_behind(x, axis, by):
-    count = lax.axis_size(axis)
-    pairs = [(i, i + by) for i in range(count) if 0 <= i + by < count]
-    return lax.ppermute(x, axis, pairs)
-
-
-def rms_scale(values, gain):
-    mean_sq = jnp.mean(values * values, axis=-1, keepdims=True)
-    return values * lax.rsqrt(mean_sq + norm_eps) * gain
-
-
-def rotate(tensor, positions):
-    half_dim = tensor.shape[-1] // 2
-    freqs = rope_theta ** (-(jnp.arange(half_dim, dtype=jnp.float32) * 2.0 / tensor.shape[-1]))
+
+
+def shards(
+    tokens, attn_gain, query_weight, keyval_weight, sink_logits, out_weight,
+    mlp_gain, routes, gate_fixed, gate_weight, up_weight, down_weight,
+):
+    ctx_index = lax.axis_index("ctx")
+    shard_len = tokens.shape[0] * lax.axis_size("fsdp")
+    half_dim = HEAD_DIM // 2
+    freqs = rope_theta ** (-(jnp.arange(half_dim, dtype=jnp.float32) * 2.0 / HEAD_DIM))
+    positions = (ctx_index * shard_len + jnp.arange(shard_len, dtype=jnp.int32)).astype(jnp.float32)
     angles = positions[:, None] * freqs[None, :]
-    cosine = jnp.cos(angles)[:, None, :]
-    sine = jnp.sin(angles)[:, None, :]
-    first = tensor[..., :half_dim]
-    second = tensor[..., half_dim:]
-    return jnp.concatenate(
-        [first * cosine - second * sine, second * cosine + first * sine], axis=-1
+    cosine = jnp.tile(jnp.cos(angles), (1, 4))
+    sine = jnp.sin(angles)
+    sine = jnp.concatenate([-sine, sine, -sine, sine], axis=1)
+    high = gate_fixed // 256
+    meta = jnp.concatenate([routes, high, gate_fixed - high * 256], axis=1).astype(jnp.float32)
+    meta = jnp.pad(meta, ((0, 0), (64, 64 - meta.shape[1])))
+    weights = (query_weight, keyval_weight, out_weight.T, gate_weight, up_weight, down_weight)
+    return layer(
+        tokens, attn_gain[None, :], jnp.pad(mlp_gain, (0, 64))[None, :],
+        cosine, sine, sink_logits, meta, weights,
     )
-
-
-def shards(
-    tokens,
-    attn_gain,
-    query_weight,
-    keyval_weight,
-    sink_logits,
-    out_weight,
-    mlp_gain,
-    routes,
-    gate_fixed,
-    gate_weight,
-    up_weight,
-    down_weight,
-):
-    ctx_size = lax.axis_size("ctx")
-    fsdp_size = lax.axis_size("fsdp")
-    ctx_index = lax.axis_index("ctx")
-    fsdp_index = lax.axis_index("fsdp")
-    local_rows = tokens.shape[0]
-    width = tokens.shape[1]
-    shard_len = local_rows * fsdp_size
-    heads_here = query_weight.shape[1] // HEAD_DIM
-    kv_blocks = keyval_weight.shape[0] // HEAD_DIM
-    block_ids = fsdp_index * kv_blocks + jnp.arange(kv_blocks, dtype=jnp.int32)
-    rope_flag = jnp.concatenate(
-        [jnp.ones((heads_here,), jnp.float32), (block_ids < KV_HEADS).astype(jnp.float32)]
-    )
-    piece = lax.all_gather(tokens, "fsdp", axis=0, tiled=True)
-    count = piece.shape[0]
-    normed = rms_scale(piece.astype(jnp.float32), attn_gain).astype(jnp.bfloat16)
-    query_val = jnp.dot(normed, query_weight, preferred_element_type=jnp.float32)
-    kv_val = lax.dot_general(
-        normed, keyval_weight, (((1,), (1,)), ((), ())), preferred_element_type=jnp.float32
-    )
-    mixed = jnp.concatenate([query_val, kv_val], axis=1).reshape(
-        count, heads_here + kv_blocks, HEAD_DIM
-    )
-    positions = (ctx_index * shard_len + jnp.arange(count, dtype=jnp.int32)).astype(jnp.float32)
-    turned = rotate(mixed, positions)
-    chosen = jnp.where(rope_flag[None, :, None] > 0.5, turned, mixed)
-    projected = chosen.astype(jnp.bfloat16).reshape(count, (heads_here + kv_blocks) * HEAD_DIM)
-    query_part = projected[:, : heads_here * HEAD_DIM].reshape(shard_len, heads_here, HEAD_DIM)
-    kv_mine = projected[:, heads_here * HEAD_DIM :]
-    own_head = fsdp_index * heads_here // (HEADS // KV_HEADS)
-    kv_all = lax.all_gather(kv_mine, "fsdp", axis=1, tiled=True)
-    key_cols = lax.dynamic_slice_in_dim(kv_all, own_head * HEAD_DIM, HEAD_DIM, 1)
-    value_cols = lax.dynamic_slice_in_dim(
-        kv_all, KV_HEADS * HEAD_DIM + own_head * HEAD_DIM, HEAD_DIM, 1
-    )
-    own_rows = jnp.concatenate([key_cols, value_cols], axis=1)
-    rim_rows = from_behind(own_rows[shard_len - WINDOW :], "ctx", 1)
-    extended = jnp.concatenate([rim_rows, own_rows], axis=0)
-    key_ext = extended[:, :HEAD_DIM]
-    value_ext = extended[:, HEAD_DIM:]
-    scores = jnp.einsum(
-        "rhd,kd->hrk", query_part, key_ext, preferred_element_type=jnp.float32
-    ) * HEAD_DIM ** (-0.5)
-    query_pos = ctx_index * shard_len + jnp.arange(shard_len, dtype=jnp.int32)
-    key_pos = ctx_index * shard_len - WINDOW + jnp.arange(shard_len + WINDOW, dtype=jnp.int32)
-    allowed = (
-        (key_pos[None, :] <= query_pos[:, None])
-        & (key_pos[None, :] > query_pos[:, None] - WINDOW)
-        & (key_pos[None, :] >= 0)
-    )
-    masked = jnp.where(allowed[None], scores, -1e30)
-    top_score = jnp.maximum(jnp.max(masked, axis=-1), sink_logits[:, None])
-    expd = jnp.exp(masked - top_score[..., None])
-    total = jnp.exp(sink_logits[:, None] - top_score) + jnp.sum(expd, axis=-1)
-    probs = (expd / total[..., None]).astype(jnp.bfloat16)
-    attended = jnp.einsum("hrk,kd->rhd", probs, value_ext, preferred_element_type=jnp.float32)
-    attended = attended.astype(jnp.bfloat16).reshape(shard_len, heads_here * HEAD_DIM)
-    attn_delta = lax.psum_scatter(
-        jnp.dot(attended, out_weight, preferred_element_type=jnp.float32).astype(jnp.bfloat16),
-        "fsdp",
-        scatter_dimension=0,
-        tiled=True,
-    ).astype(jnp.float32)
-    resid = tokens.astype(jnp.float32) + attn_delta
-    ffn_in = rms_scale(resid, mlp_gain).astype(jnp.bfloat16)
-    high = gate_fixed // 256
-    meta = jnp.concatenate([routes, high, gate_fixed - high * 256], axis=1).astype(jnp.bfloat16)
-    xin = jnp.concatenate(
-        [ffn_in, meta, jnp.zeros((local_rows, 2944 - width - meta.shape[1]), jnp.bfloat16)], axis=1
-    )
-    return moe(xin, resid, gate_weight, up_weight, down_weight)
 
 
 def solution(mesh):

time: 275 us -> 158 us (0.57)
  waiting for transfers between devices: 110 us -> 0 us
  Pallas kernels: 97.5 us -> 136 us
  blocking collectives: 22.8 us -> 0 us
  between operations: 13.7 us -> 0.05 us
  matrix products: 5.68 us -> 0 us
  local copies, waits for them, and re-layouts: 12.8 us -> 17.3 us
  other arithmetic: 5.58 us -> 1.47 us
  starting transfers between devices: 3.15 us -> 0 us
    reduce_scatter x1 -> x0, waiting for transfers between devices: 56.9 us -> none  [shards(): lax.psum_scatter(jnp.dot(attended, out_weight, preferred_element_type=jnp...]
    all_gather x1 -> x0, waiting for transfers between devices: 52 us -> none  [shards(): piece = lax.all_gather(tokens, 'fsdp', axis=0, tiled=True)]
    pallas_call x1, Pallas kernels: 97.5 us -> 136 us  [layer(): pl.pallas_call(layer_kernel, out_shape=jax.ShapeDtypeStruct(tokens.shape,...]
    all_gather x1 -> x0, blocking collectives: 22.8 us -> none  [shards(): kv_all = lax.all_gather(kv_mine, 'fsdp', axis=1, tiled=True)]
    dot_general x5 -> x0, matrix products: 5.68 us -> none  [the longest x1 2.2 us: shards(): lax.dot_general(normed, keyval_weight, (((1,), (1,)), ((), ())), preferre...]
    ppermute x1 -> x0, starting transfers between devices: 3.11 us -> none  [from_behind(): return lax.ppermute(x, axis, pairs)]
    unnamed x33 -> x14, local copies, waits for them, and re-layouts: 11.8 us -> 13.2 us
  transfers between devices with their start and end apart: 3 -> 0, of which waited for: 3 -> 0; matrix products, arithmetic and copies ran while one was open for 4% -> 0% of each run, Pallas kernels for 0% -> 0%
where the time goes in v3:
time: 158 us; the launch traced here: 155 us
  Pallas kernels  136 us (86%)
  local copies, waits for them, and re-layouts  17.3 us (11%)
    pallas_call x1, Pallas kernels, layer(): pl.pallas_call(layer_kernel, out_shape=jax.ShapeDtypeStruct(tokens.shape,...  136 us
    unnamed x14, local copies, waits for them, and re-layouts  13.2 us

profile of v3, /device:TPU:1, one launch (start us, length us, event | category | flops | bytes accessed | tf_op | source)
XLA Modules:
  0.0 155.0 jit_solution(13365903405410977293)
XLA Ops:
  0.0 0.8 copy.40
  0.8 0.8 copy.35
  1.6 0.1 add_convert_fusion
  1.6 0.7 pad.9.meta
  2.3 1.3 broadcast_in_dim.8.attn_gain
  3.6 0.7 pad.8
  4.3 0.6 broadcast_in_dim.9.mlp_gain
  4.9 0.5 fusion
  5.5 0.8 pad_maximum_fusion.sin_ref
  6.3 0.1 copy.34
  6.4 0.0 slice-start
  6.4 0.8 copy.41.cos_ref
  7.2 0.0 slice-start.1
  7.2 0.0 slice-start.2
  7.2 5.0 %copy.42.gate_hbm = bf16[4,180,2880]{2,1,0:T(8,128)(2,1)} copy(bf16[4,180,2880]{2,0,1:T(4,128)(2,1)} %param.21) | data formatting | bytes 8294400 | tf_op args[9]
  12.2 0.0 slice-done
  12.2 0.0 slice-done.1
  12.2 0.0 slice-start.3
  12.2 2.5 %copy.43.up_hbm = bf16[4,180,2880]{2,1,0:T(8,128)(2,1)} copy(bf16[4,180,2880]{2,0,1:T(4,128)(2,1)S(1)} %bitcast.3) | data formatting | bytes 8294400 | tf_op args[10]
  14.7 0.0 slice-done.2
  14.7 0.0 slice-done.3
  14.7 2.5 %copy.44.down_hbm = bf16[4,180,2880]{2,1,0:T(8,128)(2,1)} copy(bf16[4,180,2880]{2,0,1:T(4,128)(2,1)S(1)} %bitcast.5) | data formatting | bytes 8294400 | tf_op args[11]
  17.3 136.2 %layer.1 = bf16[16,2880]{1,0:T(8,128)(2,1)} custom-call(bf16[16,2880]{1,0:T(8,128)(2,1)} %tokens.1, f32[1,2880]{1,0:T(1,128)} %broadcast_in_dim.8.attn_gain, f32[1,2944]{1,0:T(1,128)} %broadcast_in_dim.9.mlp_gain, f32[256,128]{1,0:T(8,128)} %copy.41.cos_ref, f32[256,128]{1,0:T(8,128)} %pad_maximum_fusion.sin_ref, f32[4]{0:T(128)} %sinks.1, ...), custom_call_target="tpu_custom_call" | custom-call | tf_op jit(solution)/shard_map/layer/pallas_call | solution.py:582
  153.4 1.5 copy.46
  (6 shorter events, 0.0 us)
Async XLA Ops:
  6.4 5.8 %slice-start = ((s8[4239360]{0:T(1024)(128)(4,1)}), s8[45056]{0:T(1024)(128)(4,1)S(1)}, s32[]{:S(2)}) async-start(s8[4239360]{0:T(1024)(128)(4,1)} %bitcast.2), calls=%async_computation | async-start | bytes 90112
  7.2 5.0 %slice-start.1 = ((s8[4239360]{0:T(1024)(128)(4,1)}), s8[4194304]{0:T(1024)(128)(4,1)S(1)}, s32[]{:S(2)}) async-start(s8[4239360]{0:T(1024)(128)(4,1)} %bitcast.2), calls=%async_computation.1 | async-start | bytes 8388608
  7.2 7.6 %slice-start.2 = ((s8[4239360]{0:T(1024)(128)(4,1)}), s8[4194304]{0:T(1024)(128)(4,1)S(1)}, s32[]{:S(2)}) async-start(s8[4239360]{0:T(1024)(128)(4,1)} %bitcast.4), calls=%async_computation.2 | async-start | bytes 8388608
  12.2 2.5 %slice-start.3 = ((s8[4239360]{0:T(1024)(128)(4,1)}), s8[45056]{0:T(1024)(128)(4,1)S(1)}, s32[]{:S(2)}) async-start(s8[4239360]{0:T(1024)(128)(4,1)} %bitcast.4), calls=%async_computation.3 | async-start | bytes 90112

commit v4 on v3

--- a/solution.py
+++ b/solution.py
@@ -1,4 +1,4 @@
-import functools
+import math
 import jax
 import jax.numpy as jnp
 from jax import lax
@@ -14,10 +14,10 @@
 
 
 def layer_kernel(
-    tokens, attn_gain, mlp_gain, cos_ref, sin_ref, sinks, meta,
+    tokens, attn_gain, mlp_gain, sinks, routes, fixed,
     query_hbm, keyval_hbm, outw_hbm, gate_hbm, up_hbm, down_hbm, out,
     x0, x1, x2, d0, d1, d2, s0, s1, s2,
-    gate_w, up_w, down_w, table, lower,
+    gate_w, up_w, down_w, stage, hidden_all, gain_pad, table, lower,
     ra0, ra1, ra2, rb0, rb1, rb2, rc0, rc1, rc2,
     query_w, keyval_w, outw_w, gathered, normed, kv_mine, kv_all, queries, attended,
     part, part_sib, part_in, part_last, resid,
@@ -50,23 +50,48 @@
 
     loads = [
         pltpu.make_async_copy(h, v, wsem.at[i])
-        for i, (h, v) in enumerate(
-            (
-                (keyval_hbm, keyval_w), (query_hbm, query_w), (outw_hbm, outw_w),
-                (gate_hbm, gate_w), (up_hbm, up_w), (down_hbm, down_w),
-            )
-        )
+        for i, (h, v) in enumerate(((keyval_hbm, keyval_w), (query_hbm, query_w), (outw_hbm, outw_w)))
     ]
     for w in loads:
         w.start()
-    weights = loads[3:]
+
+    def chunk(i):
+        src = (gate_hbm, up_hbm, down_hbm)[i // 4]
+        n = 36 if i % 4 == 3 else 48
+        return pltpu.make_async_copy(
+            src.at[pl.ds((i % 4) * 48, n)], stage.at[i % 2, pl.ds(0, n)], wsem.at[3 + i % 2]
+        )
+
+    turned = [0]
+
+    def turn_weights(count):
+        for i in range(turned[0], min(turned[0] + count, 12)):
+            chunk(i).wait()
+            dst = (gate_w, up_w, down_w)[i // 4]
+            rows = pl.ds((i % 4) * 48, 48)
+            if i % 4 == 3:
+                stage[i % 2, 36:48] = jnp.zeros((12, 4, 2880), jnp.bfloat16)
+
+            def tile(t, _):
+                cols = pl.ds(pl.multiple_of(t * 256, 256), 256)
+                dst[:, rows, cols] = jnp.swapaxes(stage[i % 2, :, :, cols], 0, 1)
+                return 0
+
+            lax.fori_loop(0, 11, tile, 0)
+            dst[:, rows, 2816:2880] = jnp.swapaxes(stage[i % 2, :, :, 2816:2880], 0, 1)
+            if i + 2 < 12:
+                chunk(i + 2).start()
+            turned[0] = i + 1
+
+    chunk(0).start()
+    chunk(1).start()
 
     def signal(to):
         pl.semaphore_signal(barrier, inc=1, device_id=to, device_id_type=pl.DeviceIdType.MESH)
 
     barrier = pltpu.get_barrier_semaphore()
-    across = device(me[0], (me[1] + 2) % 4, me[2], core)
-    partners = [neighbour(a, b) for a in range(3) for b in (1, -1)] + [sibling, across]
+    across = neighbour(1, 2)
+    partners = [neighbour(a, b) for a in range(3) for b in (1, -1, 2)] + [sibling]
     for to in partners:
         signal(to)
     behind = (ctx + 7) % 8
@@ -122,7 +147,12 @@
         v = gathered[y_, x_, which].astype(jnp.float32)
         scale = lax.rsqrt(jnp.sum(v * v, axis=-1, keepdims=True) * (1.0 / 2880.0) + 1e-05)
         row = ((y_ * 4 + x_) * 2 + which) * 16
-        normed[pl.ds(pl.multiple_of(row, 16), 16), :] = (v * scale * attn_gain[...]).astype(jnp.bfloat16)
+        normed[pl.ds(pl.multiple_of(row, 16), 16), :] = (v * scale * attn_gain[...].reshape(1, 2880)).astype(jnp.bfloat16)
+
+    lanes = lax.broadcasted_iota(jnp.int32, (256, 128), 1)
+    early = lanes % 64 < 32
+    freqs = jnp.exp((lanes % 32).astype(jnp.float32) * (-2.0 / 64 * math.log(150000.0)))
+    angles = (ctx * 256 + lax.broadcasted_iota(jnp.int32, (256, 128), 0)).astype(jnp.float32) * freqs
 
     send(held(0, 0, core), held(0, 0, core), ta_send.at[0, 10], ta_recv.at[0, 10], across)
     for b in range(2):
@@ -135,6 +165,10 @@
         pass_on(b, 0, 0, 3, left)
         to_sibling(b, 0, 6)
         norm_block(b, 0, core)
+        if b == 0:
+            cosine = jnp.cos(angles)
+            sine = jnp.sin(angles)
+            sine = jnp.where(early, -sine, sine)
     for b in range(2):
         arrived(b, -1, 0, 0)
         pass_on(b, -1, 0, 4, right)
@@ -159,8 +193,6 @@
             norm_block(b, by, 1 - core)
 
     nt = (((1,), (1,)), ((), ()))
-    cosine, sine = cos_ref[...], sin_ref[...]
-    early = lax.broadcasted_iota(jnp.int32, (256, 128), 1) % 64 < 32
 
     def turn(v, c_, s_):
         return v * c_ + jnp.where(early, pltpu.roll(v, 96, 1), pltpu.roll(v, 32, 1)) * s_
@@ -291,90 +323,145 @@
     resid[:, 0:2880] = tokens[...].astype(jnp.float32) + total
     v = resid[...]
     scale = lax.rsqrt(jnp.sum(v * v, axis=-1, keepdims=True) * (1.0 / 2880.0) + 1e-05)
-    v = v * scale * mlp_gain[...]
+    gain_pad[...] = jnp.zeros((1, 2944), jnp.float32)
+    gain_pad[:, 0:2880] = mlp_gain[...].reshape(1, 2880)
+    v = v * scale * gain_pad[...]
+    high = fixed[...] // 256
+    low = fixed[...] - high * 256
+    meta = jnp.concatenate([routes[...], high, low, jnp.zeros((4, 16), jnp.int32)], axis=0)
+    meta = meta.astype(jnp.float32).T.astype(jnp.bfloat16)
+    spot = lax.broadcasted_iota(jnp.int32, (16, 128), 0) + 64 == lax.broadcasted_iota(jnp.int32, (16, 128), 1)
+    meta = jnp.dot(meta, jnp.where(spot, 1.0, 0.0).astype(jnp.bfloat16), preferred_element_type=jnp.float32)
     for p, (lo, n, wide) in enumerate(PARTS):
         w = v[:, lo : lo + wide]
         if p == 2:
-            w = jnp.concatenate([w[:, :768], w[:, 768:] + meta[...]], axis=1)
+            w = jnp.concatenate([w[:, :768], w[:, 768:] + meta], axis=1)
         xs[p][me[0], me[1], me[2], core] = w.astype(jnp.bfloat16)
     for cp in started:
         cp.wait_send()
 
-    def view(ref, p, stage, by, cols, which=None):
-        axis = ORDERS[p][stage]
-        free = ORDERS[p][:stage]
-        idx = []
-        for a in range(3):
-            if a in free:
-                idx.append(slice(None))
-            elif a == axis:
-                idx.append((me[a] + by + 4) % 4)
-            else:
-                idx.append(me[a])
-        if which is not None:
-            idx.append(which)
-        return ref.at[tuple(idx) + (slice(None), cols)]
-
-    def halves(p):
-        return pl.ds(0, HALF), pl.ds(HALF, PARTS[p][2] - HALF)
-
-    def whole(p):
-        return pl.ds(0, PARTS[p][2])
+    ALL = "all"
+
+    def where_(p, offsets, drop=()):
+        idx = [None] * 3
+        for s, o in enumerate(offsets):
+            a = ORDERS[p][s]
+            idx[a] = slice(None) if o is ALL else (me[a] + o + 4) % 4
+        return tuple(idx[a] for a in range(3) if a not in [ORDERS[p][s] for s in drop])
+
+    def cols_of(p, half):
+        if half is None:
+            return pl.ds(0, PARTS[p][2])
+        return (pl.ds(0, HALF), pl.ds(HALF, PARTS[p][2] - HALF))[half]
+
+    def mine(p, offsets, half=None, which=None):
+        which = core if which is None else which
+        return xs[p].at[where_(p, offsets) + (which, slice(None), cols_of(p, half))]
+
+    def ways(p, s):
+        return neighbour(ORDERS[p][s], 1), neighbour(ORDERS[p][s], -1)
 
     pending = []
-    for p in range(3):
-        v = view(xs[p], p, 0, 0, whole(p), core)
-        cp = copy(v, v, sib_send.at[p, 0, 3], sib_recv.at[p, 0, 3], sibling)
+
+    def ag(p, k, v, to):
+        cp = copy(v, v, ag_send.at[p, k], ag_recv.at[p, k], to)
         cp.start()
         pending.append(cp)
 
-    def ag(p, st, by, half, k, to):
-        v = view(xs[p], p, st, by, halves(p)[half], core)
-        cp = copy(v, v, ag_send.at[p, st, k], ag_recv.at[p, st, k], to)
+    def ag_wait(p, k, v):
+        copy(v, v, ag_send.at[p, k], ag_recv.at[p, k], sibling).wait_recv()
+
+    forwards = []
+
+    def forward(p, offsets):
+        k = len([f for f in forwards if f[0] == p])
+        forwards.append((p, k, offsets))
+        v = mine(p, offsets)
+        cp = copy(v, v, sib_send.at[p, k], sib_recv.at[p, k], sibling)
         cp.start()
         pending.append(cp)
 
-    def ag_wait(p, st, by, half, k):
-        v = view(xs[p], p, st, by, halves(p)[half], core)
-        copy(v, v, ag_send.at[p, st, k], ag_recv.at[p, st, k], sibling).wait_recv()
-
-    def forward(p, st, by, k):
-        v = view(xs[p], p, st, by, whole(p), core)
-        cp = copy(v, v, sib_send.at[p, st, k], sib_recv.at[p, st, k], sibling)
-        cp.start()
-        pending.append(cp)
-
-    for st in range(3):
-        for p in range(3):
-            a = ORDERS[p][st]
-            up, dn = neighbour(a, 1), neighbour(a, -1)
-            ag(p, st, 0, 0, 0, up)
-            ag(p, st, 0, 1, 1, dn)
-            ag(p, st, 0, 1, 2, up)
-            ag(p, st, 0, 0, 3, dn)
-        for p in range(3):
-            a = ORDERS[p][st]
-            up, dn = neighbour(a, 1), neighbour(a, -1)
-            ag_wait(p, st, -1, 0, 0)
-            ag(p, st, -1, 0, 4, up)
-            ag_wait(p, st, 1, 1, 1)
-            ag(p, st, 1, 1, 5, dn)
-        for p in range(3):
-            ag_wait(p, st, -1, 1, 2)
-            forward(p, st, -1, 0)
-            ag_wait(p, st, 1, 0, 3)
-            forward(p, st, 1, 1)
-        for p in range(3):
-            ag_wait(p, st, 2, 0, 4)
-            ag_wait(p, st, 2, 1, 5)
-            forward(p, st, 2, 2)
-    for p in range(3):
-        v = view(xs[p], p, 0, 0, whole(p), 1 - core)
-        copy(v, v, sib_send.at[p, 0, 3], sib_recv.at[p, 0, 3], sibling).wait_recv()
-        for st in range(3):
-            for k, by in enumerate((-1, 1, 2)):
-                v = view(xs[p], p, st, by, whole(p), 1 - core)
-                copy(v, v, sib_send.at[p, st, k], sib_recv.at[p, st, k], sibling).wait_recv()
+    def third(p, j):
+        up, dn = ways(p, 2)
+        k = 9 + (j % 4) * 4
+        ag(p, k, mine(p, (ALL, j, 0)), up)
+        ag(p, k + 1, mine(p, (ALL, j, 0)), dn)
+
+    def third_relay(p, j):
+        up, dn = ways(p, 2)
+        k = 9 + (j % 4) * 4
+        ag_wait(p, k, mine(p, (ALL, j, -1)))
+        ag(p, k + 2, mine(p, (ALL, j, -1), 0), up)
+        ag_wait(p, k + 1, mine(p, (ALL, j, 1)))
+        ag(p, k + 3, mine(p, (ALL, j, 1), 1), dn)
+        forward(p, (ALL, j, -1))
+        forward(p, (ALL, j, 1))
+
+    def third_end(p, j):
+        k = 9 + (j % 4) * 4
+        ag_wait(p, k + 2, mine(p, (ALL, j, 2), 0))
+        ag_wait(p, k + 3, mine(p, (ALL, j, 2), 1))
+        forward(p, (ALL, j, 2))
+
+    for p in range(3):
+        own = mine(p, (0, 0, 0))
+        up, dn = ways(p, 0)
+        ag(p, 0, own, up)
+        ag(p, 1, own, dn)
+        ag(p, 2, own, neighbour(ORDERS[p][0], 2))
+    turn_weights(2)
+    for p in range(3):
+        ag_wait(p, 0, mine(p, (-1, 0, 0)))
+        ag_wait(p, 1, mine(p, (1, 0, 0)))
+        ag_wait(p, 2, mine(p, (2, 0, 0)))
+        up, dn = ways(p, 1)
+        ag(p, 3, mine(p, (ALL, 0, 0), 0), up)
+        ag(p, 4, mine(p, (ALL, 0, 0), 1), dn)
+        ag(p, 5, mine(p, (ALL, 0, 0), 1), up)
+        ag(p, 6, mine(p, (ALL, 0, 0), 0), dn)
+        third(p, 0)
+        forward(p, (ALL, 0, 0))
+    turn_weights(2)
+    for p in range(3):
+        up, dn = ways(p, 1)
+        ag_wait(p, 3, mine(p, (ALL, -1, 0), 0))
+        ag(p, 7, mine(p, (ALL, -1, 0), 0), up)
+        ag_wait(p, 4, mine(p, (ALL, 1, 0), 1))
+        ag(p, 8, mine(p, (ALL, 1, 0), 1), dn)
+    for p in range(3):
+        ag_wait(p, 5, mine(p, (ALL, -1, 0), 1))
+        third(p, -1)
+        ag_wait(p, 6, mine(p, (ALL, 1, 0), 0))
+        third(p, 1)
+        forward(p, (ALL, -1, 0))
+        forward(p, (ALL, 1, 0))
+    turn_weights(1)
+    for p in range(3):
+        third_relay(p, 0)
+    turn_weights(1)
+    for p in range(3):
+        ag_wait(p, 7, mine(p, (ALL, 2, 0), 0))
+        ag_wait(p, 8, mine(p, (ALL, 2, 0), 1))
+        third(p, 2)
+        forward(p, (ALL, 2, 0))
+    turn_weights(1)
+    for p in range(3):
+        third_end(p, 0)
+        third_relay(p, -1)
+    turn_weights(2)
+    for p in range(3):
+        third_relay(p, 1)
+        third_end(p, -1)
+    turn_weights(2)
+    for p in range(3):
+        third_relay(p, 2)
+        third_end(p, 1)
+    turn_weights(12)
+    for p in range(3):
+        third_end(p, 2)
+    for p, k, offsets in forwards:
+        v = mine(p, offsets, None, 1 - core)
+        copy(v, v, sib_send.at[p, k], sib_recv.at[p, k], sibling).wait_recv()
     for cp in pending:
         cp.wait_send()
 
@@ -409,142 +496,185 @@
 
     lax.fori_loop(0, GROUPS, dispatch, 0)
 
-    for w in weights:
-        w.wait()
-
     def expert(e, _):
-        gate = jnp.zeros((256, 180), jnp.float32)
-        upv = jnp.zeros((256, 180), jnp.float32)
+        gate = jnp.zeros((256, 192), jnp.float32)
+        upv = jnp.zeros((256, 192), jnp.float32)
         for p, (lo, n, held) in enumerate(PARTS):
             y = ds[p][e, :, 0:n]
-            nt = (((1,), (1,)), ((), ()))
             gate = gate + lax.dot_general(y, gate_w[e, :, lo : lo + n], nt, preferred_element_type=jnp.float32)
             upv = upv + lax.dot_general(y, up_w[e, :, lo : lo + n], nt, preferred_element_type=jnp.float32)
-        meta = ds[2][e, :, 768:896].astype(jnp.float32)
+        about = ds[2][e, :, 768:896].astype(jnp.float32)
         weight = jnp.zeros((256, 1), jnp.float32)
         number = (first_expert + e).astype(jnp.float32)
         for k in range(4):
-            value = meta[:, 68 + k : 69 + k] * 256.0 + meta[:, 72 + k : 73 + k]
-            weight = weight + jnp.where(meta[:, 64 + k : 65 + k] == number, value, 0.0)
+            value = about[:, 68 + k : 69 + k] * 256.0 + about[:, 72 + k : 73 + k]
+            weight = weight + jnp.where(about[:, 64 + k : 65 + k] == number, value, 0.0)
         hidden = gate * jax.nn.sigmoid(GLU * gate) * (upv + 1.0)
-        hidden = (hidden * (weight * (1.0 / 65536.0))).astype(jnp.bfloat16)
-        for p, (lo, n, held) in enumerate(PARTS):
+        hidden_all[e] = (hidden * (weight * (1.0 / 65536.0))).astype(jnp.bfloat16)
+        return 0
+
+    lax.fori_loop(0, 4, expert, 0)
+
+    pending = []
+    turns = (2, 1, -1, 0)
+
+    def other(p, offsets):
+        return ss[p].at[where_(p, offsets)]
+
+    def land3(p, slot, j, half=None):
+        return rbufs[p][2].at[(slot,) + where_(p, (ALL, j, 0), (2,)) + (slice(None), cols_of(p, half))]
+
+    def land2(p, slot, half=None):
+        return rbufs[p][1].at[slot, :, :, cols_of(p, half)]
+
+    def rs(p, k, src, dst, to):
+        cp = copy(src, dst, rs_send.at[p, k], rs_recv.at[p, k], to)
+        cp.start()
+        pending.append(cp)
+
+    def rs_wait(p, k, dst):
+        copy(dst, dst, rs_send.at[p, k], rs_recv.at[p, k], sibling).wait_recv()
+
+    def add(dst, *others):
+        def one(i, _):
+            total = dst[i].astype(jnp.float32)
+            for o in others:
+                total = total + o[i].astype(jnp.float32)
+            dst[i] = total.astype(jnp.bfloat16)
+            return 0
+
+        lax.fori_loop(0, 4, one, 0)
+
+    def half_of(ref, p, half):
+        return ref.at[:, :, cols_of(p, half)]
+
+    def first(p, j):
+        v = other(p, (ALL, j, ALL))
+        copy(v, v, sx_send.at[p, j % 4], sx_recv.at[p, j % 4], sibling).wait_recv()
+        up, dn = ways(p, 2)
+        k = 9 + (j % 4) * 4
+        add(mine(p, (ALL, j, 2)), other(p, (ALL, j, 2)))
+        rs(p, k, mine(p, (ALL, j, 2), 0), land3(p, 2, j, 0), up)
+        rs(p, k + 1, mine(p, (ALL, j, 2), 1), land3(p, 2, j, 1), dn)
+
+    def mid(p, j):
+        up, dn = ways(p, 2)
+        k = 9 + (j % 4) * 4
+        add(mine(p, (ALL, j, 1), 1), half_of(other(p, (ALL, j, 1)), p, 1))
+        add(mine(p, (ALL, j, -1), 0), half_of(other(p, (ALL, j, -1)), p, 0))
+        rs_wait(p, k, land3(p, 2, j, 0))
+        add(mine(p, (ALL, j, 1), 0), half_of(other(p, (ALL, j, 1)), p, 0), land3(p, 2, j, 0))
+        rs(p, k + 2, mine(p, (ALL, j, 1)), land3(p, 0, j), up)
+        rs_wait(p, k + 1, land3(p, 2, j, 1))
+        add(mine(p, (ALL, j, -1), 1), half_of(other(p, (ALL, j, -1)), p, 1), land3(p, 2, j, 1))
+        rs(p, k + 3, mine(p, (ALL, j, -1)), land3(p, 1, j), dn)
+
+    def last(p, j):
+        k = 9 + (j % 4) * 4
+        rs_wait(p, k + 2, land3(p, 0, j))
+        rs_wait(p, k + 3, land3(p, 1, j))
+        add(mine(p, (ALL, j, 0)), other(p, (ALL, j, 0)), land3(p, 0, j), land3(p, 1, j))
+        up, dn = ways(p, 1)
+        if j == 2:
+            rs(p, 3, mine(p, (ALL, 2, 0), 0), land2(p, 2, 0), up)
+            rs(p, 4, mine(p, (ALL, 2, 0), 1), land2(p, 2, 1), dn)
+        if j == 1:
+            rs(p, 5, mine(p, (ALL, 1, 0), 1), land2(p, 0, 1), up)
+        if j == -1:
+            rs(p, 6, mine(p, (ALL, -1, 0), 0), land2(p, 1, 0), dn)
+
+    def second(p):
+        up, dn = ways(p, 1)
+        rs_wait(p, 3, land2(p, 2, 0))
+        add(mine(p, (ALL, 1, 0), 0), land2(p, 2, 0))
+        rs(p, 7, mine(p, (ALL, 1, 0), 0), land2(p, 0, 0), up)
+        rs_wait(p, 4, land2(p, 2, 1))
+        add(mine(p, (ALL, -1, 0), 1), land2(p, 2, 1))
+        rs(p, 8, mine(p, (ALL, -1, 0), 1), land2(p, 1, 1), dn)
+
+    def second_end(p):
+        rs_wait(p, 5, land2(p, 0, 1))
+        rs_wait(p, 6, land2(p, 1, 0))
+        rs_wait(p, 7, land2(p, 0, 0))
+        rs_wait(p, 8, land2(p, 1, 1))
+        add(mine(p, (ALL, 0, 0)), land2(p, 0), land2(p, 1))
+        up, dn = ways(p, 0)
+        rs(p, 0, mine(p, (1, 0, 0)), rbufs[p][0].at[0], up)
+        rs(p, 1, mine(p, (-1, 0, 0)), rbufs[p][0].at[1], dn)
+        rs(p, 2, mine(p, (2, 0, 0)), rbufs[p][0].at[2], neighbour(ORDERS[p][0], 2))
+
+    def produce(p):
+        lo, n, wide = PARTS[p]
+
+        def down(e, _):
             ds[p][e, :, 0:n] = jnp.dot(
-                hidden, down_w[e, :, lo : lo + n], preferred_element_type=jnp.float32
+                hidden_all[e], down_w[e, :, lo : lo + n], preferred_element_type=jnp.float32
             ).astype(jnp.bfloat16)
-        return 0
-
-    lax.fori_loop(0, 4, expert, 0)
-
-    pending = []
-    for p in range(3):
-        n = PARTS[p][1]
-
-        def combine(g, _, p=p, n=n):
-            z, yh = g // 2, g % 2
+            return 0
+
+        lax.fori_loop(0, 4, down, 0)
+
+        def combine(g, _):
+            z, yh_ = g // 2, g % 2
             y = jnp.concatenate([ds[p][e, pl.ds(g * 32, 32), :] for e in range(4)], axis=0)
             got = jnp.dot(table[g], y, preferred_element_type=jnp.float32).astype(jnp.bfloat16)
-            xs[p][z, pl.ds(yh * 2, 2)] = got.reshape(2, 4, 2, 16, PARTS[p][2])
+            xs[p][z, pl.ds(yh_ * 2, 2)] = got.reshape(2, 4, 2, 16, wide)
             return 0
 
         lax.fori_loop(0, GROUPS, combine, 0)
-        for k, by in enumerate((2, 1, -1, 0)):
+        for j in turns:
             cp = copy(
-                view(xs[p], p, 2, by, whole(p), 1 - core), view(ss[p], p, 2, by, whole(p)),
-                sx_send.at[p, k], sx_recv.at[p, k], sibling,
+                mine(p, (ALL, j, ALL), None, 1 - core), other(p, (ALL, j, ALL)),
+                sx_send.at[p, j % 4], sx_recv.at[p, j % 4], sibling,
             )
             cp.start()
             pending.append(cp)
 
-    def add(dst, *others):
-        lead = dst.shape[:-2]
-        count = 1
-        for s in lead:
-            count *= s
-
-        def one(i, _):
-            idx = () if not lead else ((i,) if len(lead) == 1 else (i // 4, i % 4))
-            total = dst[idx].astype(jnp.float32)
-            for o in others:
-                total = total + o[idx].astype(jnp.float32)
-            dst[idx] = total.astype(jnp.bfloat16)
-            return 0
-
-        if lead:
-            lax.fori_loop(0, count, one, 0)
-        else:
-            one(0, 0)
-
-    def rs(p, st, k, src, dst, to):
-        cp = copy(src, dst, rs_send.at[p, st, k], rs_recv.at[p, st, k], to)
-        cp.start()
-        pending.append(cp)
-
-    def rs_wait(p, st, k, dst):
-        copy(dst, dst, rs_send.at[p, st, k], rs_recv.at[p, st, k], sibling).wait_recv()
-
-    def sib_wait(p, k, by):
-        v = view(ss[p], p, 2, by, whole(p))
-        copy(v, v, sx_send.at[p, k], sx_recv.at[p, k], sibling).wait_recv()
-
-    for st in (2, 1, 0):
-        for p in range(3):
-            a = ORDERS[p][st]
-            up, dn = neighbour(a, 1), neighbour(a, -1)
-            ha, hb = halves(p)
-            r = rbufs[p][st]
-            if st == 2:
-                sib_wait(p, 0, 2)
-                add(view(xs[p], p, st, 2, whole(p), core), view(ss[p], p, st, 2, whole(p)))
-            rs(p, st, 0, view(xs[p], p, st, 2, ha, core), r.at[2, ..., ha], up)
-            rs(p, st, 1, view(xs[p], p, st, 2, hb, core), r.at[2, ..., hb], dn)
-        for p in range(3):
-            a = ORDERS[p][st]
-            up, dn = neighbour(a, 1), neighbour(a, -1)
-            ha, hb = halves(p)
-            r = rbufs[p][st]
-            if st == 2:
-                sib_wait(p, 1, 1)
-                add(view(xs[p], p, st, 1, whole(p), core), view(ss[p], p, st, 1, whole(p)))
-            rs(p, st, 2, view(xs[p], p, st, 1, hb, core), r.at[0, ..., hb], up)
-            if st == 2:
-                sib_wait(p, 2, -1)
-                add(view(xs[p], p, st, -1, whole(p), core), view(ss[p], p, st, -1, whole(p)))
-            rs(p, st, 3, view(xs[p], p, st, -1, ha, core), r.at[1, ..., ha], dn)
-        for p in range(3):
-            a = ORDERS[p][st]
-            up, dn = neighbour(a, 1), neighbour(a, -1)
-            ha, hb = halves(p)
-            r = rbufs[p][st]
-            rs_wait(p, st, 0, r.at[2, ..., ha])
-            add(view(xs[p], p, st, 1, ha, core), r.at[2, ..., ha])
-            rs(p, st, 4, view(xs[p], p, st, 1, ha, core), r.at[0, ..., ha], up)
-            rs_wait(p, st, 1, r.at[2, ..., hb])
-            add(view(xs[p], p, st, -1, hb, core), r.at[2, ..., hb])
-            rs(p, st, 5, view(xs[p], p, st, -1, hb, core), r.at[1, ..., hb], dn)
-        for p in range(3):
-            ha, hb = halves(p)
-            r = rbufs[p][st]
-            own = view(xs[p], p, st, 0, whole(p), core)
-            others = [r.at[0], r.at[1]]
-            if st == 2:
-                sib_wait(p, 3, 0)
-                others.append(view(ss[p], p, st, 0, whole(p)))
-            rs_wait(p, st, 2, r.at[0, ..., hb])
-            rs_wait(p, st, 3, r.at[1, ..., ha])
-            rs_wait(p, st, 4, r.at[0, ..., ha])
-            rs_wait(p, st, 5, r.at[1, ..., hb])
-            if st:
-                add(own, *others)
-            else:
-                lo, n, held = PARTS[p]
-                total = own[...].astype(jnp.float32) + r[0].astype(jnp.float32) + r[1].astype(jnp.float32)
-                out[:, lo : lo + n] = (resid[:, lo : lo + n] + total[:, :n]).astype(jnp.bfloat16)
+    produce(0)
+    produce(1)
+    first(0, 2)
+    first(0, 1)
+    produce(2)
+    first(1, 2)
+    first(1, 1)
+    first(0, -1)
+    first(0, 0)
+    mid(0, 2)
+    first(2, 2)
+    first(2, 1)
+    mid(1, 2)
+    first(1, -1)
+    first(1, 0)
+    mid(0, 1)
+    mid(2, 2)
+    first(2, -1)
+    first(2, 0)
+    mid(1, 1)
+    mid(2, 1)
+    for p in range(3):
+        last(p, 2)
+        mid(p, -1)
+    for p in range(3):
+        last(p, 1)
+        mid(p, 0)
+    for p in range(3):
+        last(p, -1)
+        second(p)
+    for p in range(3):
+        last(p, 0)
+    for p in range(3):
+        second_end(p)
+    for p, (lo, n, wide) in enumerate(PARTS):
+        total = mine(p, (0, 0, 0))[...].astype(jnp.float32)
+        for s in range(3):
+            rs_wait(p, s, rbufs[p][0].at[s])
+            total = total + rbufs[p][0][s].astype(jnp.float32)
+        out[:, lo : lo + n] = (resid[:, lo : lo + n] + total[:, :n]).astype(jnp.bfloat16)
     for cp in pending:
         cp.wait_send()
 
 
-def layer(tokens, attn_gain, mlp_gain, cosine, sine, sinks, meta, weights):
+def layer(tokens, attn_gain, mlp_gain, sinks, routes, fixed, weights):
     bf = jnp.bfloat16
     wide = [p[2] for p in PARTS]
     width = tokens.shape[1]
@@ -553,7 +683,12 @@
         [pltpu.VMEM((4, 4, 4, 2, 16, h), bf) for h in wide]
         + [pltpu.VMEM((4, 256, h), bf) for h in wide]
         + [pltpu.VMEM((4, 4, 4, 16, h), bf) for h in wide]
-        + [pltpu.VMEM(w.shape, bf) for w in weights[3:]]
+        + [pltpu.VMEM((4, 192, width), bf)] * 3
+        + [
+            pltpu.VMEM((2, 48, 4, width), bf),
+            pltpu.VMEM((4, 256, 192), bf),
+            pltpu.VMEM((1, 2944), jnp.float32),
+        ]
         + [pltpu.VMEM((GROUPS, 256, 128), bf), pltpu.VMEM((256, 256), bf)]
         + [pltpu.VMEM((3,) + (4,) * s + (16, h), bf) for h in wide for s in range(3)]
         + [pltpu.VMEM(w.shape, bf) for w in (weights[0], weights[1], weights[2])]
@@ -571,8 +706,8 @@
             pltpu.VMEM((16, 2944), jnp.float32),
         ]
         + [
-            dma((6,)), dma((3, 3, 6)), dma((3, 3, 6)), dma((3, 3, 4)), dma((3, 3, 4)),
-            dma((3, 3, 6)), dma((3, 3, 6)), dma((3, 4)), dma((3, 4)),
+            dma((5,)), dma((3, 25)), dma((3, 25)), dma((3, 16)), dma((3, 16)),
+            dma((3, 25)), dma((3, 25)), dma((3, 4)), dma((3, 4)),
             dma((2, 11)), dma((2, 11)), dma((4,)), dma((4,)), dma((11,)), dma((11,)),
         ]
     )
@@ -582,41 +717,23 @@
     return pl.pallas_call(
         layer_kernel,
         out_shape=jax.ShapeDtypeStruct(tokens.shape, bf),
-        in_specs=[vm] * 5 + [sm, vm] + [anym] * 6,
+        in_specs=[vm] * 3 + [sm] + [vm] * 2 + [anym] * 6,
         out_specs=vm,
         scratch_shapes=scratch,
         compiler_params=pltpu.CompilerParams(
             collective_id=1, has_side_effects=True, vmem_limit_bytes=62 * 1024 * 1024
         ),
         name="layer",
-    )(tokens, attn_gain, mlp_gain, cosine, sine, sinks, meta, *weights)
-
-
-HEAD_DIM = 64
-rope_theta = 150000.0
+    )(tokens, attn_gain, mlp_gain, sinks, routes, fixed, *weights)
 
 
 def shards(
     tokens, attn_gain, query_weight, keyval_weight, sink_logits, out_weight,
     mlp_gain, routes, gate_fixed, gate_weight, up_weight, down_weight,
 ):
-    ctx_index = lax.axis_index("ctx")
-    shard_len = tokens.shape[0] * lax.axis_size("fsdp")
-    half_dim = HEAD_DIM // 2
-    freqs = rope_theta ** (-(jnp.arange(half_dim, dtype=jnp.float32) * 2.0 / HEAD_DIM))
-    positions = (ctx_index * shard_len + jnp.arange(shard_len, dtype=jnp.int32)).astype(jnp.float32)
-    angles = positions[:, None] * freqs[None, :]
-    cosine = jnp.tile(jnp.cos(angles), (1, 4))
-    sine = jnp.sin(angles)
-    sine = jnp.concatenate([-sine, sine, -sine, sine], axis=1)
-    high = gate_fixed // 256
-    meta = jnp.concatenate([routes, high, gate_fixed - high * 256], axis=1).astype(jnp.float32)
-    meta = jnp.pad(meta, ((0, 0), (64, 64 - meta.shape[1])))
-    weights = (query_weight, keyval_weight, out_weight.T, gate_weight, up_weight, down_weight)
-    return layer(
-        tokens, attn_gain[None, :], jnp.pad(mlp_gain, (0, 64))[None, :],
-        cosine, sine, sink_logits, meta, weights,
-    )
+    experts = [jnp.transpose(w, (1, 0, 2)) for w in (gate_weight, up_weight, down_weight)]
+    weights = (query_weight, keyval_weight, out_weight.T, *experts)
+    return layer(tokens, attn_gain, mlp_gain, sink_logits, routes.T, gate_fixed.T, weights)
 
 
 def solution(mesh):

time: 158 us -> 134 us (0.85); the launches traced: 155 us -> 133 us
  local copies, waits for them, and re-layouts: 17.3 us -> 1.54 us
  Pallas kernels: 136 us -> 131 us
    unnamed x14 -> x1, local copies, waits for them, and re-layouts: 13.2 us -> 1.54 us
    pallas_call x1, Pallas kernels: 136 us -> 131 us  [layer(): pl.pallas_call(layer_kernel, out_shape=jax.ShapeDtypeStruct(tokens.shape,...]
    broadcast_in_dim x2 -> x0, local copies, waits for them, and re-layouts: 1.92 us -> none  [the longest x1 1.31 us: shards(): attn_gain[None, :]]
where the time goes in v4:
time: 134 us; the launch traced here: 133 us
  Pallas kernels  131 us (98%)
  local copies, waits for them, and re-layouts  1.54 us (1%)
    pallas_call x1, Pallas kernels, layer(): pl.pallas_call(layer_kernel, out_shape=jax.ShapeDtypeStruct(tokens.shape,...  131 us

profile of v4, /device:TPU:1, one launch (start us, length us, event | category | flops | bytes accessed | tf_op | source)
XLA Modules:
  0.0 133.0 jit_solution(16617054567733654080)
XLA Ops:
  0.0 131.5 %layer.1 = bf16[16,2880]{1,0:T(8,128)(2,1)} custom-call(bf16[16,2880]{1,0:T(8,128)(2,1)} %tokens.1, f32[2880]{0:T(1024)} %attn_gain.1, f32[2880]{0:T(1024)} %mlp_gain.1, f32[4]{0:T(128)} %sinks.1, s32[4,16]{1,0:T(4,128)} %bitcast.10, s32[4,16]{1,0:T(4,128)} %bitcast.11, bf16[2880,256]{1,0:T(8,128)(2,1)} %query_hbm.1, bf16[64,2880]{1,0:T(8,128)(2,1)} %keyval_hbm.1, ...), custom_call_target="tpu_custom_call" | custom-call | tf_op jit(solution)/shard_map/layer/pallas_call | solution.py:717
  131.5 1.5 %copy.14 = bf16[16,2880]{1,0:T(8,128)(2,1)} copy(bf16[16,2880]{1,0:T(8,128)(2,1)} %layer.1) | data formatting | bytes 184320

commit v5 on v4

--- a/solution.py
+++ b/solution.py
@@ -29,15 +29,16 @@
     rbufs = ((ra0, ra1, ra2), (rb0, rb1, rb2), (rc0, rc1, rc2))
     ctx = lax.axis_index("ctx")
     fsdp = lax.axis_index("fsdp")
-    core = fsdp % 2
-    me = (ctx // 2, (fsdp // 8) * 2 + ctx % 2, (fsdp // 2) % 4)
+    core = lax.rem(fsdp, 2)
+    me = (lax.div(ctx, 2), lax.div(fsdp, 8) * 2 + lax.rem(ctx, 2), lax.rem(lax.div(fsdp, 2), 4))
+    shifted = [[me[a]] + [lax.rem(me[a] + by, 4) for by in (1, 2, 3)] for a in range(3)]
 
     def device(z, y, x, c):
-        return (z * 2 + y % 2, ((y // 2) * 4 + x) * 2 + c)
+        return (z * 2 + lax.rem(y, 2), (lax.div(y, 2) * 4 + x) * 2 + c)
 
     def neighbour(axis, by):
         at = list(me)
-        at[axis] = (at[axis] + by + 4) % 4
+        at[axis] = shifted[axis][by % 4]
         return device(*at, core)
 
     sibling = device(*me, 1 - core)
@@ -91,7 +92,8 @@
 
     barrier = pltpu.get_barrier_semaphore()
     across = neighbour(1, 2)
-    partners = [neighbour(a, b) for a in range(3) for b in (1, -1, 2)] + [sibling]
+    diagonal = [device(me[0], shifted[1][2], shifted[2][by % 4], core) for by in range(4)]
+    partners = [neighbour(a, b) for a in range(3) for b in (1, -1, 2)] + [sibling] + diagonal[1:]
     for to in partners:
         signal(to)
     behind = (ctx + 7) % 8
@@ -108,7 +110,8 @@
     def _():
         signal((ctx, value_from))
 
-    yh = me[1] // 2
+    yh = lax.div(me[1], 2)
+    ys = (yh, 1 - yh)
     gathered[yh, me[2], core] = tokens[...]
     r = lax.broadcasted_iota(jnp.int32, (256, 256), 0)
     c = lax.broadcasted_iota(jnp.int32, (256, 256), 1)
@@ -126,24 +129,11 @@
     left, right = neighbour(2, -1), neighbour(2, 1)
     halves_of = (pl.ds(0, 1408), pl.ds(1408, 1472))
 
-    def held(b, by, which, half=None):
-        at = gathered.at[(yh + b) % 2, (me[2] + by + 4) % 4, which]
-        return at if half is None else at.at[:, halves_of[half]]
-
-    def pass_on(b, by, half, k, to):
-        v = held(b, by, core, half)
-        send(v, v, ta_send.at[b, k], ta_recv.at[b, k], to)
-
-    def arrived(b, by, half, k):
-        v = held(b, by, core, half)
-        copy(v, v, ta_send.at[b, k], ta_recv.at[b, k], sibling).wait_recv()
-
-    def to_sibling(b, by, k):
-        v = held(b, by, core)
-        send(v, v, ta_send.at[b, k], ta_recv.at[b, k], sibling)
+    def held(b, by, which):
+        return gathered.at[ys[b], shifted[2][by % 4], which]
 
     def norm_block(b, by, which):
-        y_, x_ = (yh + b) % 2, (me[2] + by + 4) % 4
+        y_, x_ = ys[b], shifted[2][by % 4]
         v = gathered[y_, x_, which].astype(jnp.float32)
         scale = lax.rsqrt(jnp.sum(v * v, axis=-1, keepdims=True) * (1.0 / 2880.0) + 1e-05)
         row = ((y_ * 4 + x_) * 2 + which) * 16
@@ -154,42 +144,26 @@
     freqs = jnp.exp((lanes % 32).astype(jnp.float32) * (-2.0 / 64 * math.log(150000.0)))
     angles = (ctx * 256 + lax.broadcasted_iota(jnp.int32, (256, 128), 0)).astype(jnp.float32) * freqs
 
-    send(held(0, 0, core), held(0, 0, core), ta_send.at[0, 10], ta_recv.at[0, 10], across)
+    mates = ((1, 2), (1, 1), (1, -1), (0, 2), (1, 0), (0, 1), (0, -1))
+    own = held(0, 0, core)
+    for b, by in mates:
+        to = diagonal[by % 4] if b else neighbour(2, by)
+        copy(own, own, ta_send.at[0], ta_recv.at[b * 4 + by % 4], to).start()
+    copy(own, own, ta_send.at[1], ta_recv.at[8], sibling).start()
+    norm_block(0, 0, core)
+    cosine = jnp.cos(angles)
+    sine = jnp.sin(angles)
+    sine = jnp.where(early, -sine, sine)
+    turn_weights(4)
+    for b, by in ((0, -1), (0, 1), (1, 0), (0, 2), (1, -1), (1, 1), (1, 2)):
+        v = held(b, by, core)
+        copy(v, v, ta_send.at[0], ta_recv.at[b * 4 + -by % 4], sibling).wait_recv()
+        copy(v, v, ta_send.at[1], ta_recv.at[8], sibling).start()
+        norm_block(b, by, core)
+    v = gathered.at[:, :, 1 - core]
+    copy(v, v, ta_send.at[1], ta_recv.at[8], sibling).wait_recv()
     for b in range(2):
-        if b == 1:
-            v = held(1, 0, core)
-            copy(v, v, ta_send.at[0, 10], ta_recv.at[0, 10], sibling).wait_recv()
-        pass_on(b, 0, 0, 0, right)
-        pass_on(b, 0, 1, 1, left)
-        pass_on(b, 0, 1, 2, right)
-        pass_on(b, 0, 0, 3, left)
-        to_sibling(b, 0, 6)
-        norm_block(b, 0, core)
-        if b == 0:
-            cosine = jnp.cos(angles)
-            sine = jnp.sin(angles)
-            sine = jnp.where(early, -sine, sine)
-    for b in range(2):
-        arrived(b, -1, 0, 0)
-        pass_on(b, -1, 0, 4, right)
-        arrived(b, 1, 1, 1)
-        pass_on(b, 1, 1, 5, left)
-    for b in range(2):
-        arrived(b, -1, 1, 2)
-        to_sibling(b, -1, 7)
-        arrived(b, 1, 0, 3)
-        to_sibling(b, 1, 8)
-        norm_block(b, -1, core)
-        norm_block(b, 1, core)
-    for b in range(2):
-        arrived(b, 2, 0, 4)
-        arrived(b, 2, 1, 5)
-        to_sibling(b, 2, 9)
-        norm_block(b, 2, core)
-    for k, by in ((6, 0), (7, -1), (8, 1), (9, 2)):
-        for b in range(2):
-            v = held(b, by, 1 - core)
-            copy(v, v, ta_send.at[b, k], ta_recv.at[b, k], sibling).wait_recv()
+        for by in range(4):
             norm_block(b, by, 1 - core)
 
     nt = (((1,), (1,)), ((), ()))
@@ -228,6 +202,7 @@
     for i in range(2):
         cols = slice(i * 128, i * 128 + 128)
         queries[:, cols] = turn(query[:, cols], cosine, sine).astype(jnp.bfloat16)
+    turn_weights(1)
     for w in range(2):
         v = kv_all.at[w, main]
 
@@ -270,13 +245,13 @@
 
     def piece(by, half=None):
         cols = slice(None) if half is None else halves_of[half]
-        return part.at[:, (me[2] + by + 4) % 4, core, :, cols]
+        return part.at[:, shifted[2][by % 4], core, :, cols]
 
     def landed(slot, half):
         return part_in.at[slot, :, :, halves_of[half]]
 
     def from_sibling(by):
-        return part_sib.at[:, (me[2] + by + 4) % 4]
+        return part_sib.at[:, shifted[2][by % 4]]
 
     def tr_wait(k, v):
         copy(v, v, tr_send.at[k], tr_recv.at[k], sibling).wait_recv()
@@ -290,9 +265,10 @@
 
     for k, by in enumerate((2, 1, -1, 0)):
         send(
-            part.at[:, (me[2] + by + 4) % 4, 1 - core], from_sibling(by),
+            part.at[:, shifted[2][by % 4], 1 - core], from_sibling(by),
             tr_send.at[k], tr_recv.at[k], sibling,
         )
+    turn_weights(1)
     tr_wait(0, from_sibling(2))
     plus(piece(2), from_sibling(2))
     send(piece(2, 0), landed(2, 0), tr_send.at[4], tr_recv.at[4], right)
@@ -303,6 +279,7 @@
     tr_wait(2, from_sibling(-1))
     plus(piece(-1), from_sibling(-1))
     send(piece(-1, 0), landed(1, 0), tr_send.at[7], tr_recv.at[7], left)
+    turn_weights(2)
     tr_wait(4, landed(2, 0))
     plus(piece(1, 0), landed(2, 0))
     send(piece(1, 0), landed(0, 0), tr_send.at[8], tr_recv.at[8], right)
@@ -311,12 +288,14 @@
     send(piece(-1, 1), landed(1, 1), tr_send.at[9], tr_recv.at[9], left)
     tr_wait(3, from_sibling(0))
     plus(piece(0), from_sibling(0))
+    turn_weights(2)
     tr_wait(6, landed(0, 1))
     tr_wait(7, landed(1, 0))
     tr_wait(8, landed(0, 0))
     tr_wait(9, landed(1, 1))
     plus(piece(0), part_in.at[0], part_in.at[1])
     send(part.at[1 - yh, me[2], core], part_last, tr_send.at[10], tr_recv.at[10], across)
+    turn_weights(12)
     tr_wait(10, part_last)
     total = part[yh, me[2], core].astype(jnp.float32) + part_last[...].astype(jnp.float32)
     resid[:, 2816:2944] = jnp.zeros((16, 128), jnp.float32)
@@ -337,6 +316,10 @@
         if p == 2:
             w = jnp.concatenate([w[:, :768], w[:, 768:] + meta], axis=1)
         xs[p][me[0], me[1], me[2], core] = w.astype(jnp.bfloat16)
+    v = gathered.at[:, :, core]
+    copy(v, v, ta_send.at[1], ta_recv.at[8], sibling).wait_send()
+    for v in (gathered.at[yh, :, core], gathered.at[yh, pl.ds(0, 3), core]):
+        copy(v, v, ta_send.at[0], ta_recv.at[8], sibling).wait_send()
     for cp in started:
         cp.wait_send()
 
@@ -346,7 +329,7 @@
         idx = [None] * 3
         for s, o in enumerate(offsets):
             a = ORDERS[p][s]
-            idx[a] = slice(None) if o is ALL else (me[a] + o + 4) % 4
+            idx[a] = slice(None) if o is ALL else shifted[a][o % 4]
         return tuple(idx[a] for a in range(3) if a not in [ORDERS[p][s] for s in drop])
 
     def cols_of(p, half):
@@ -361,25 +344,21 @@
     def ways(p, s):
         return neighbour(ORDERS[p][s], 1), neighbour(ORDERS[p][s], -1)
 
-    pending = []
-
     def ag(p, k, v, to):
-        cp = copy(v, v, ag_send.at[p, k], ag_recv.at[p, k], to)
-        cp.start()
-        pending.append(cp)
+        copy(v, v, ag_send.at[p], ag_recv.at[p, k], to).start()
 
     def ag_wait(p, k, v):
-        copy(v, v, ag_send.at[p, k], ag_recv.at[p, k], sibling).wait_recv()
-
-    forwards = []
+        copy(v, v, ag_send.at[p], ag_recv.at[p, k], sibling).wait_recv()
 
     def forward(p, offsets):
-        k = len([f for f in forwards if f[0] == p])
-        forwards.append((p, k, offsets))
         v = mine(p, offsets)
-        cp = copy(v, v, sib_send.at[p, k], sib_recv.at[p, k], sibling)
-        cp.start()
-        pending.append(cp)
+        copy(v, v, sib_send.at[p], sib_recv.at[p], sibling).start()
+
+    def wait_sent(p, sem):
+        some = pl.ds(0, 3)
+        for idx in ((some,), (0, some), (0, 0, some)):
+            v = xs[p].at[idx + (slice(None),) * (3 - len(idx)) + (core,)]
+            copy(v, v, sem, ag_recv.at[p, 0], sibling).wait_send()
 
     def third(p, j):
         up, dn = ways(p, 2)
@@ -409,7 +388,6 @@
         ag(p, 0, own, up)
         ag(p, 1, own, dn)
         ag(p, 2, own, neighbour(ORDERS[p][0], 2))
-    turn_weights(2)
     for p in range(3):
         ag_wait(p, 0, mine(p, (-1, 0, 0)))
         ag_wait(p, 1, mine(p, (1, 0, 0)))
@@ -421,7 +399,6 @@
         ag(p, 6, mine(p, (ALL, 0, 0), 0), dn)
         third(p, 0)
         forward(p, (ALL, 0, 0))
-    turn_weights(2)
     for p in range(3):
         up, dn = ways(p, 1)
         ag_wait(p, 3, mine(p, (ALL, -1, 0), 0))
@@ -435,35 +412,27 @@
         third(p, 1)
         forward(p, (ALL, -1, 0))
         forward(p, (ALL, 1, 0))
-    turn_weights(1)
     for p in range(3):
         third_relay(p, 0)
-    turn_weights(1)
     for p in range(3):
         ag_wait(p, 7, mine(p, (ALL, 2, 0), 0))
         ag_wait(p, 8, mine(p, (ALL, 2, 0), 1))
         third(p, 2)
         forward(p, (ALL, 2, 0))
-    turn_weights(1)
     for p in range(3):
         third_end(p, 0)
         third_relay(p, -1)
-    turn_weights(2)
     for p in range(3):
         third_relay(p, 1)
         third_end(p, -1)
-    turn_weights(2)
     for p in range(3):
         third_relay(p, 2)
         third_end(p, 1)
-    turn_weights(12)
     for p in range(3):
         third_end(p, 2)
-    for p, k, offsets in forwards:
-        v = mine(p, offsets, None, 1 - core)
-        copy(v, v, sib_send.at[p, k], sib_recv.at[p, k], sibling).wait_recv()
-    for cp in pending:
-        cp.wait_send()
+    for p in range(3):
+        v = mine(p, (ALL, ALL, ALL), None, 1 - core)
+        copy(v, v, sib_send.at[p], sib_recv.at[p], sibling).wait_recv()
 
     first_expert = fsdp * 4
     lane = lax.broadcasted_iota(jnp.int32, (256, 128), 1)
@@ -515,7 +484,6 @@
 
     lax.fori_loop(0, 4, expert, 0)
 
-    pending = []
     turns = (2, 1, -1, 0)
 
     def other(p, offsets):
@@ -528,29 +496,24 @@
         return rbufs[p][1].at[slot, :, :, cols_of(p, half)]
 
     def rs(p, k, src, dst, to):
-        cp = copy(src, dst, rs_send.at[p, k], rs_recv.at[p, k], to)
-        cp.start()
-        pending.append(cp)
+        copy(src, dst, rs_send.at[p], rs_recv.at[p, k], to).start()
 
     def rs_wait(p, k, dst):
-        copy(dst, dst, rs_send.at[p, k], rs_recv.at[p, k], sibling).wait_recv()
+        copy(dst, dst, rs_send.at[p], rs_recv.at[p, k], sibling).wait_recv()
 
     def add(dst, *others):
-        def one(i, _):
-            total = dst[i].astype(jnp.float32)
+        for i in range(4):
+            total = dst[i]
             for o in others:
-                total = total + o[i].astype(jnp.float32)
-            dst[i] = total.astype(jnp.bfloat16)
-            return 0
-
-        lax.fori_loop(0, 4, one, 0)
+                total = total + o[i]
+            dst[i] = total
 
     def half_of(ref, p, half):
         return ref.at[:, :, cols_of(p, half)]
 
     def first(p, j):
         v = other(p, (ALL, j, ALL))
-        copy(v, v, sx_send.at[p, j % 4], sx_recv.at[p, j % 4], sibling).wait_recv()
+        copy(v, v, sx_send.at[p], sx_recv.at[p, j % 4], sibling).wait_recv()
         up, dn = ways(p, 2)
         k = 9 + (j % 4) * 4
         add(mine(p, (ALL, j, 2)), other(p, (ALL, j, 2)))
@@ -605,6 +568,9 @@
 
     def produce(p):
         lo, n, wide = PARTS[p]
+        wait_sent(p, ag_send.at[p])
+        v = mine(p, (ALL, ALL, ALL))
+        copy(v, v, sib_send.at[p], sib_recv.at[p], sibling).wait_send()
 
         def down(e, _):
             ds[p][e, :, 0:n] = jnp.dot(
@@ -623,12 +589,10 @@
 
         lax.fori_loop(0, GROUPS, combine, 0)
         for j in turns:
-            cp = copy(
+            copy(
                 mine(p, (ALL, j, ALL), None, 1 - core), other(p, (ALL, j, ALL)),
-                sx_send.at[p, j % 4], sx_recv.at[p, j % 4], sibling,
-            )
-            cp.start()
-            pending.append(cp)
+                sx_send.at[p], sx_recv.at[p, j % 4], sibling,
+            ).start()
 
     produce(0)
     produce(1)
@@ -670,8 +634,10 @@
             rs_wait(p, s, rbufs[p][0].at[s])
             total = total + rbufs[p][0][s].astype(jnp.float32)
         out[:, lo : lo + n] = (resid[:, lo : lo + n] + total[:, :n]).astype(jnp.bfloat16)
-    for cp in pending:
-        cp.wait_send()
+    for p in range(3):
+        wait_sent(p, rs_send.at[p])
+        v = other(p, (ALL, ALL, ALL))
+        copy(v, v, sx_send.at[p], sx_recv.at[p, 0], sibling).wait_send()
 
 
 def layer(tokens, attn_gain, mlp_gain, sinks, routes, fixed, weights):
@@ -706,9 +672,9 @@
             pltpu.VMEM((16, 2944), jnp.float32),
         ]
         + [
-            dma((5,)), dma((3, 25)), dma((3, 25)), dma((3, 16)), dma((3, 16)),
-            dma((3, 25)), dma((3, 25)), dma((3, 4)), dma((3, 4)),
-            dma((2, 11)), dma((2, 11)), dma((4,)), dma((4,)), dma((11,)), dma((11,)),
+            dma((5,)), dma((3,)), dma((3, 25)), dma((3,)), dma((3,)),
+            dma((3,)), dma((3, 25)), dma((3,)), dma((3, 4)),
+            dma((2,)), dma((9,)), dma((4,)), dma((4,)), dma((11,)), dma((11,)),
         ]
     )
     vm = pl.BlockSpec(memory_space=pltpu.VMEM)

time: 134 us -> 132 us (0.985)
    pallas_call x1, Pallas kernels: 131 us -> 130 us  [layer(): pl.pallas_call(layer_kernel, out_shape=jax.ShapeDtypeStruct(tokens.shape,...]
where the time goes in v5:
time: 132 us
  Pallas kernels  130 us (98%)
  local copies, waits for them, and re-layouts  1.54 us (1%)
    pallas_call x1, Pallas kernels, layer(): pl.pallas_call(layer_kernel, out_shape=jax.ShapeDtypeStruct(tokens.shape,...  130 us

profile of v5, /device:TPU:1, one launch (start us, length us, event | category | flops | bytes accessed | tf_op | source)
XLA Modules:
  0.0 131.6 jit_solution(4597106647969708133)
XLA Ops:
  0.0 130.0 %layer.1 = bf16[16,2880]{1,0:T(8,128)(2,1)} custom-call(bf16[16,2880]{1,0:T(8,128)(2,1)} %tokens.1, f32[2880]{0:T(1024)} %attn_gain.1, f32[2880]{0:T(1024)} %mlp_gain.1, f32[4]{0:T(128)} %sinks.1, s32[4,16]{1,0:T(4,128)} %bitcast.10, s32[4,16]{1,0:T(4,128)} %bitcast.11, bf16[2880,256]{1,0:T(8,128)(2,1)} %query_hbm.1, bf16[64,2880]{1,0:T(8,128)(2,1)} %keyval_hbm.1, ...), custom_call_target="tpu_custom_call" | custom-call | tf_op jit(solution)/shard_map/layer/pallas_call | solution.py:683
  130.0 1.5 %copy.14 = bf16[16,2880]{1,0:T(8,128)(2,1)} copy(bf16[16,2880]{1,0:T(8,128)(2,1)} %layer.1) | data formatting | bytes 184320

commit v6 on v5

--- a/solution.py
+++ b/solution.py
@@ -17,13 +17,13 @@
     tokens, attn_gain, mlp_gain, sinks, routes, fixed,
     query_hbm, keyval_hbm, outw_hbm, gate_hbm, up_hbm, down_hbm, out,
     x0, x1, x2, d0, d1, d2, s0, s1, s2,
-    gate_w, up_w, down_w, stage, hidden_all, gain_pad, table, lower,
+    gate_w, up_w, down_w, stage, hidden_all, gain_pad, table, picks, slot_weight, metas, lower,
     ra0, ra1, ra2, rb0, rb1, rb2, rc0, rc1, rc2,
     query_w, keyval_w, outw_w, gathered, normed, kv_mine, kv_all, queries, attended,
     part, part_sib, part_in, part_last, resid,
     wsem, ag_send, ag_recv, sib_send, sib_recv,
     rs_send, rs_recv, sx_send, sx_recv,
-    ta_send, ta_recv, kv_send, kv_recv, tr_send, tr_recv,
+    mt_send, mt_recv, ta_send, ta_recv, kv_send, kv_recv, tr_send, tr_recv,
 ):
     xs, ds, ss = (x0, x1, x2), (d0, d1, d2), (s0, s1, s2)
     rbufs = ((ra0, ra1, ra2), (rb0, rb1, rb2), (rc0, rc1, rc2))
@@ -113,6 +113,14 @@
     yh = lax.div(me[1], 2)
     ys = (yh, 1 - yh)
     gathered[yh, me[2], core] = tokens[...]
+    high = fixed[...] // 256
+    low = fixed[...] - high * 256
+    about = jnp.concatenate([routes[...], high, low, jnp.zeros((4, 16), jnp.int32)], axis=0)
+    about = about.astype(jnp.float32).T.astype(jnp.bfloat16)
+    spot = lax.broadcasted_iota(jnp.int32, (16, 128), 0) == lax.broadcasted_iota(jnp.int32, (16, 128), 1)
+    about = jnp.dot(about, jnp.where(spot, 1.0, 0.0).astype(jnp.bfloat16), preferred_element_type=jnp.float32)
+    metas[me[0], me[1], me[2], core] = about.astype(jnp.bfloat16)
+
     r = lax.broadcasted_iota(jnp.int32, (256, 256), 0)
     c = lax.broadcasted_iota(jnp.int32, (256, 256), 1)
     lower[...] = jnp.where((r // 16 == c // 16) & (c < r), 1.0, 0.0).astype(jnp.bfloat16)
@@ -144,22 +152,39 @@
     freqs = jnp.exp((lanes % 32).astype(jnp.float32) * (-2.0 / 64 * math.log(150000.0)))
     angles = (ctx * 256 + lax.broadcasted_iota(jnp.int32, (256, 128), 0)).astype(jnp.float32) * freqs
 
+    def meta_view(stage, by):
+        idx = tuple(slice(None) if a < stage else (shifted[a][by % 4] if a == stage else me[a]) for a in range(3))
+        return metas.at[idx + (core,)]
+
+    def meta_send(stage):
+        v = meta_view(stage, 0)
+        for by in (2, 1, -1):
+            copy(v, v, mt_send.at[0], mt_recv.at[stage * 4 + by % 4], neighbour(stage, by)).start()
+
+    def meta_wait(stage):
+        for by in (2, 1, -1):
+            v = meta_view(stage, by)
+            copy(v, v, mt_send.at[0], mt_recv.at[stage * 4 + -by % 4], sibling).wait_recv()
+
     mates = ((1, 2), (1, 1), (1, -1), (0, 2), (1, 0), (0, 1), (0, -1))
     own = held(0, 0, core)
     for b, by in mates:
         to = diagonal[by % 4] if b else neighbour(2, by)
         copy(own, own, ta_send.at[0], ta_recv.at[b * 4 + by % 4], to).start()
     copy(own, own, ta_send.at[1], ta_recv.at[8], sibling).start()
+    meta_send(0)
     norm_block(0, 0, core)
     cosine = jnp.cos(angles)
     sine = jnp.sin(angles)
     sine = jnp.where(early, -sine, sine)
-    turn_weights(4)
+    turn_weights(6)
     for b, by in ((0, -1), (0, 1), (1, 0), (0, 2), (1, -1), (1, 1), (1, 2)):
         v = held(b, by, core)
         copy(v, v, ta_send.at[0], ta_recv.at[b * 4 + -by % 4], sibling).wait_recv()
         copy(v, v, ta_send.at[1], ta_recv.at[8], sibling).start()
         norm_block(b, by, core)
+    meta_wait(0)
+    meta_send(1)
     v = gathered.at[:, :, 1 - core]
     copy(v, v, ta_send.at[1], ta_recv.at[8], sibling).wait_recv()
     for b in range(2):
@@ -197,6 +222,8 @@
             kv_mine.at[pl.ds(128, 128)], kv_all.at[which, rim],
             kv_send.at[2 + i], kv_recv.at[which * 2 + 1], (ahead, to),
         )
+    meta_wait(1)
+    meta_send(2)
     loads[1].wait()
     query = jnp.dot(normed[...], query_w[...], preferred_element_type=jnp.float32)
     for i in range(2):
@@ -236,6 +263,9 @@
             mixed = jnp.dot(probs, values, preferred_element_type=jnp.float32)
             attended[b * 128 : b * 128 + 128, h * 64 : h * 64 + 64] = mixed.astype(jnp.bfloat16)
 
+    meta_wait(2)
+    v = metas.at[:, :, :, core]
+    copy(v, v, mt_send.at[1], mt_recv.at[12], sibling).start()
     loads[2].wait()
     for lo, n in ((0, 1024), (1024, 1024), (2048, 832)):
         got = lax.dot_general(
@@ -243,6 +273,42 @@
         ).astype(jnp.bfloat16)
         part[:, :, :, :, lo : lo + n] = got.reshape(2, 4, 2, 16, n)
 
+    def octant(zh, yh_, xh):
+        return pl.ds(zh * 2, 2), pl.ds(yh_ * 2, 2), pl.ds(xh * 2, 2)
+
+    first_expert = fsdp * 4
+    lane = lax.broadcasted_iota(jnp.int32, (256, 128), 1)
+    row = lax.broadcasted_iota(jnp.int32, (256, 128), 0)
+    lane_expert = (first_expert + lane // 32).astype(jnp.float32)
+    lane_slot = ((lane % 32) // 16).astype(jnp.float32)
+    same_source = row // 16 == lane % 16
+    slot_expert = (first_expert + row[:128] // 32).astype(jnp.float32)
+
+    def tables(lo, hi):
+        def one(o, _):
+            known = metas[octant(o // 4, (o // 2) % 2, o % 2)].reshape(256, 128)
+            ids = known.astype(jnp.float32)
+            hit = jnp.zeros((256, 128), jnp.float32)
+            for k in range(4):
+                hit = hit + jnp.where(ids[:, k : k + 1] == lane_expert, 1.0, 0.0)
+            rank = jnp.dot(lower[...], hit.astype(jnp.bfloat16), preferred_element_type=jnp.float32)
+            t = jnp.where((rank == lane_slot) & same_source, hit, 0.0)
+            table[o] = t.astype(jnp.bfloat16)
+            pick = t.T.astype(jnp.bfloat16)
+            picks[o] = pick
+            got = jnp.dot(pick, known, preferred_element_type=jnp.float32)
+            weight = jnp.zeros((128, 128), jnp.float32)
+            for k in range(4):
+                value = got[:, 4 + k : 5 + k] * 256.0 + got[:, 8 + k : 9 + k]
+                weight = weight + jnp.where(got[:, k : k + 1] == slot_expert, value, 0.0)
+            weight = weight * (1.0 / 65536.0)
+            at = pl.ds(pl.multiple_of(o * 32, 32), 32)
+            for e in range(4):
+                slot_weight[e, at, :] = weight[e * 32 : e * 32 + 32]
+            return 0
+
+        lax.fori_loop(lo, hi, one, 0)
+
     def piece(by, half=None):
         cols = slice(None) if half is None else halves_of[half]
         return part.at[:, shifted[2][by % 4], core, :, cols]
@@ -268,7 +334,6 @@
             part.at[:, shifted[2][by % 4], 1 - core], from_sibling(by),
             tr_send.at[k], tr_recv.at[k], sibling,
         )
-    turn_weights(1)
     tr_wait(0, from_sibling(2))
     plus(piece(2), from_sibling(2))
     send(piece(2, 0), landed(2, 0), tr_send.at[4], tr_recv.at[4], right)
@@ -279,7 +344,9 @@
     tr_wait(2, from_sibling(-1))
     plus(piece(-1), from_sibling(-1))
     send(piece(-1, 0), landed(1, 0), tr_send.at[7], tr_recv.at[7], left)
-    turn_weights(2)
+    v = metas.at[:, :, :, 1 - core]
+    copy(v, v, mt_send.at[1], mt_recv.at[12], sibling).wait_recv()
+    tables(0, 5)
     tr_wait(4, landed(2, 0))
     plus(piece(1, 0), landed(2, 0))
     send(piece(1, 0), landed(0, 0), tr_send.at[8], tr_recv.at[8], right)
@@ -288,6 +355,7 @@
     send(piece(-1, 1), landed(1, 1), tr_send.at[9], tr_recv.at[9], left)
     tr_wait(3, from_sibling(0))
     plus(piece(0), from_sibling(0))
+    tables(5, 8)
     turn_weights(2)
     tr_wait(6, landed(0, 1))
     tr_wait(7, landed(1, 0))
@@ -305,21 +373,17 @@
     gain_pad[...] = jnp.zeros((1, 2944), jnp.float32)
     gain_pad[:, 0:2880] = mlp_gain[...].reshape(1, 2880)
     v = v * scale * gain_pad[...]
-    high = fixed[...] // 256
-    low = fixed[...] - high * 256
-    meta = jnp.concatenate([routes[...], high, low, jnp.zeros((4, 16), jnp.int32)], axis=0)
-    meta = meta.astype(jnp.float32).T.astype(jnp.bfloat16)
-    spot = lax.broadcasted_iota(jnp.int32, (16, 128), 0) + 64 == lax.broadcasted_iota(jnp.int32, (16, 128), 1)
-    meta = jnp.dot(meta, jnp.where(spot, 1.0, 0.0).astype(jnp.bfloat16), preferred_element_type=jnp.float32)
     for p, (lo, n, wide) in enumerate(PARTS):
         w = v[:, lo : lo + wide]
-        if p == 2:
-            w = jnp.concatenate([w[:, :768], w[:, 768:] + meta], axis=1)
         xs[p][me[0], me[1], me[2], core] = w.astype(jnp.bfloat16)
     v = gathered.at[:, :, core]
     copy(v, v, ta_send.at[1], ta_recv.at[8], sibling).wait_send()
     for v in (gathered.at[yh, :, core], gathered.at[yh, pl.ds(0, 3), core]):
         copy(v, v, ta_send.at[0], ta_recv.at[8], sibling).wait_send()
+    for v in (metas.at[pl.ds(0, 3), :, :, core], metas.at[0, pl.ds(0, 3), :, core], metas.at[0, 0, pl.ds(0, 3), core]):
+        copy(v, v, mt_send.at[0], mt_recv.at[12], sibling).wait_send()
+    v = metas.at[:, :, :, core]
+    copy(v, v, mt_send.at[1], mt_recv.at[12], sibling).wait_send()
     for cp in started:
         cp.wait_send()
 
@@ -352,10 +416,36 @@
 
     def forward(p, offsets):
         v = mine(p, offsets)
-        copy(v, v, sib_send.at[p], sib_recv.at[p], sibling).start()
+        group = 2 * (offsets[1] == 2) + (offsets[2] == 2)
+        copy(v, v, sib_send.at[p], sib_recv.at[p, group], sibling).start()
+
+    some = pl.ds(0, 3)
+    near = [lax.div(me[a], 2) for a in range(3)]
+    far = [1 - h for h in near]
+
+    def pair(p, two, three):
+        for i in range(2):
+            half = [None] * 3
+            for s, h in enumerate((i, two, three)):
+                half[ORDERS[p][s]] = h
+            yield half[0] * 4 + half[1] * 2 + half[2], octant(*half)
+
+    def halves_at(p, group):
+        a2, a3 = ORDERS[p][1:]
+        return (far if group >= 2 else near)[a2], (far if group % 2 else near)[a3]
+
+    def dispatch(p, group):
+        idx = ((some, some, slice(None)), (0, some, slice(None)), (0, some, slice(None)), (0, 0, slice(None)))[group]
+        v = xs[p].at[idx + (1 - core,)]
+        copy(v, v, sib_send.at[p], sib_recv.at[p, group], sibling).wait_recv()
+        for o, at in pair(p, *halves_at(p, group)):
+            src = xs[p][at].reshape(256, PARTS[p][2])
+            got = jnp.dot(picks[o], src, preferred_element_type=jnp.float32).astype(jnp.bfloat16)
+            to = pl.ds(pl.multiple_of(o * 32, 32), 32)
+            for e in range(4):
+                ds[p][e, to, :] = got[e * 32 : (e + 1) * 32]
 
     def wait_sent(p, sem):
-        some = pl.ds(0, 3)
         for idx in ((some,), (0, some), (0, 0, some)):
             v = xs[p].at[idx + (slice(None),) * (3 - len(idx)) + (core,)]
             copy(v, v, sem, ag_recv.at[p, 0], sibling).wait_send()
@@ -426,44 +516,18 @@
         third_relay(p, 1)
         third_end(p, -1)
     for p in range(3):
+        dispatch(p, 0)
+    for p in range(3):
         third_relay(p, 2)
         third_end(p, 1)
     for p in range(3):
+        dispatch(p, 1)
+    for p in range(3):
+        dispatch(p, 2)
+    for p in range(3):
         third_end(p, 2)
     for p in range(3):
-        v = mine(p, (ALL, ALL, ALL), None, 1 - core)
-        copy(v, v, sib_send.at[p], sib_recv.at[p], sibling).wait_recv()
-
-    first_expert = fsdp * 4
-    lane = lax.broadcasted_iota(jnp.int32, (256, 128), 1)
-    row = lax.broadcasted_iota(jnp.int32, (256, 128), 0)
-    lane_expert = (first_expert + lane // 32).astype(jnp.float32)
-    lane_slot = ((lane % 32) // 16).astype(jnp.float32)
-    same_source = row // 16 == lane % 16
-
-    def dispatch(g, _):
-        z, yh = g // 2, g % 2
-
-        def rows(p):
-            return xs[p][z, pl.ds(yh * 2, 2)].reshape(256, PARTS[p][2])
-
-        last = rows(2)
-        ids = last[:, 768:896].astype(jnp.float32)
-        hit = jnp.zeros((256, 128), jnp.float32)
-        for k in range(4):
-            hit = hit + jnp.where(ids[:, 64 + k : 65 + k] == lane_expert, 1.0, 0.0)
-        rank = jnp.dot(lower[...], hit.astype(jnp.bfloat16), preferred_element_type=jnp.float32)
-        t = jnp.where((rank == lane_slot) & same_source, hit, 0.0)
-        table[g] = t.astype(jnp.bfloat16)
-        pick = t.T.astype(jnp.bfloat16)
-        for p in range(3):
-            src = last if p == 2 else rows(p)
-            got = jnp.dot(pick, src, preferred_element_type=jnp.float32).astype(jnp.bfloat16)
-            for e in range(4):
-                ds[p][e, pl.ds(g * 32, 32), :] = got[e * 32 : (e + 1) * 32]
-        return 0
-
-    lax.fori_loop(0, GROUPS, dispatch, 0)
+        dispatch(p, 3)
 
     def expert(e, _):
         gate = jnp.zeros((256, 192), jnp.float32)
@@ -472,14 +536,8 @@
             y = ds[p][e, :, 0:n]
             gate = gate + lax.dot_general(y, gate_w[e, :, lo : lo + n], nt, preferred_element_type=jnp.float32)
             upv = upv + lax.dot_general(y, up_w[e, :, lo : lo + n], nt, preferred_element_type=jnp.float32)
-        about = ds[2][e, :, 768:896].astype(jnp.float32)
-        weight = jnp.zeros((256, 1), jnp.float32)
-        number = (first_expert + e).astype(jnp.float32)
-        for k in range(4):
-            value = about[:, 68 + k : 69 + k] * 256.0 + about[:, 72 + k : 73 + k]
-            weight = weight + jnp.where(about[:, 64 + k : 65 + k] == number, value, 0.0)
         hidden = gate * jax.nn.sigmoid(GLU * gate) * (upv + 1.0)
-        hidden_all[e] = (hidden * (weight * (1.0 / 65536.0))).astype(jnp.bfloat16)
+        hidden_all[e] = (hidden * slot_weight[e][:, 0:1]).astype(jnp.bfloat16)
         return 0
 
     lax.fori_loop(0, 4, expert, 0)
@@ -512,8 +570,6 @@
         return ref.at[:, :, cols_of(p, half)]
 
     def first(p, j):
-        v = other(p, (ALL, j, ALL))
-        copy(v, v, sx_send.at[p], sx_recv.at[p, j % 4], sibling).wait_recv()
         up, dn = ways(p, 2)
         k = 9 + (j % 4) * 4
         add(mine(p, (ALL, j, 2)), other(p, (ALL, j, 2)))
@@ -566,55 +622,65 @@
         rs(p, 1, mine(p, (-1, 0, 0)), rbufs[p][0].at[1], dn)
         rs(p, 2, mine(p, (2, 0, 0)), rbufs[p][0].at[2], neighbour(ORDERS[p][0], 2))
 
-    def produce(p):
+    def down(p):
         lo, n, wide = PARTS[p]
-        wait_sent(p, ag_send.at[p])
-        v = mine(p, (ALL, ALL, ALL))
-        copy(v, v, sib_send.at[p], sib_recv.at[p], sibling).wait_send()
-
-        def down(e, _):
+
+        def one(e, _):
             ds[p][e, :, 0:n] = jnp.dot(
                 hidden_all[e], down_w[e, :, lo : lo + n], preferred_element_type=jnp.float32
             ).astype(jnp.bfloat16)
             return 0
 
-        lax.fori_loop(0, 4, down, 0)
-
-        def combine(g, _):
-            z, yh_ = g // 2, g % 2
-            y = jnp.concatenate([ds[p][e, pl.ds(g * 32, 32), :] for e in range(4)], axis=0)
-            got = jnp.dot(table[g], y, preferred_element_type=jnp.float32).astype(jnp.bfloat16)
-            xs[p][z, pl.ds(yh_ * 2, 2)] = got.reshape(2, 4, 2, 16, wide)
-            return 0
-
-        lax.fori_loop(0, GROUPS, combine, 0)
-        for j in turns:
-            copy(
-                mine(p, (ALL, j, ALL), None, 1 - core), other(p, (ALL, j, ALL)),
-                sx_send.at[p], sx_recv.at[p, j % 4], sibling,
-            ).start()
-
-    produce(0)
-    produce(1)
+        lax.fori_loop(0, 4, one, 0)
+        wait_sent(p, ag_send.at[p])
+        v = mine(p, (ALL, ALL, ALL))
+        copy(v, v, sib_send.at[p], sib_recv.at[p, 0], sibling).wait_send()
+
+    def swap(p, group):
+        idx = [slice(None)] * 3
+        for s, h in zip((1, 2), halves_at(p, group)):
+            idx[ORDERS[p][s]] = pl.ds(h * 2, 2)
+        idx = tuple(idx)
+        return copy(
+            xs[p].at[idx + (1 - core,)], ss[p].at[idx], sx_send.at[p], sx_recv.at[p, group], sibling
+        )
+
+    def combine(p, group):
+        for o, at in pair(p, *halves_at(p, group)):
+            rows = pl.ds(pl.multiple_of(o * 32, 32), 32)
+            y = jnp.concatenate([ds[p][e, rows, :] for e in range(4)], axis=0)
+            got = jnp.dot(table[o], y, preferred_element_type=jnp.float32).astype(jnp.bfloat16)
+            xs[p][at] = got.reshape(2, 2, 2, 2, 16, PARTS[p][2])
+        swap(p, group).start()
+
+    down(0)
+    combine(0, 3)
+    down(1)
+    combine(1, 3)
+    swap(0, 3).wait_recv()
     first(0, 2)
-    first(0, 1)
-    produce(2)
+    down(2)
+    combine(2, 3)
+    swap(1, 3).wait_recv()
     first(1, 2)
-    first(1, 1)
-    first(0, -1)
-    first(0, 0)
-    mid(0, 2)
+    combine(0, 2)
+    swap(2, 3).wait_recv()
     first(2, 2)
-    first(2, 1)
-    mid(1, 2)
-    first(1, -1)
-    first(1, 0)
-    mid(0, 1)
-    mid(2, 2)
-    first(2, -1)
-    first(2, 0)
-    mid(1, 1)
-    mid(2, 1)
+    combine(1, 2)
+    combine(2, 2)
+    for p in range(3):
+        swap(p, 2).wait_recv()
+        mid(p, 2)
+        combine(p, 1)
+        combine(p, 0)
+    for p in range(3):
+        swap(p, 1).wait_recv()
+        swap(p, 0).wait_recv()
+        first(p, 1)
+        first(p, -1)
+        first(p, 0)
+    for p in range(3):
+        mid(p, 1)
     for p in range(3):
         last(p, 2)
         mid(p, -1)
@@ -655,7 +721,13 @@
             pltpu.VMEM((4, 256, 192), bf),
             pltpu.VMEM((1, 2944), jnp.float32),
         ]
-        + [pltpu.VMEM((GROUPS, 256, 128), bf), pltpu.VMEM((256, 256), bf)]
+        + [
+            pltpu.VMEM((GROUPS, 256, 128), bf),
+            pltpu.VMEM((GROUPS, 128, 256), bf),
+            pltpu.VMEM((4, 256, 128), jnp.float32),
+            pltpu.VMEM((4, 4, 4, 2, 16, 128), bf),
+            pltpu.VMEM((256, 256), bf),
+        ]
         + [pltpu.VMEM((3,) + (4,) * s + (16, h), bf) for h in wide for s in range(3)]
         + [pltpu.VMEM(w.shape, bf) for w in (weights[0], weights[1], weights[2])]
         + [
@@ -672,9 +744,9 @@
             pltpu.VMEM((16, 2944), jnp.float32),
         ]
         + [
-            dma((5,)), dma((3,)), dma((3, 25)), dma((3,)), dma((3,)),
+            dma((5,)), dma((3,)), dma((3, 25)), dma((3,)), dma((3, 4)),
             dma((3,)), dma((3, 25)), dma((3,)), dma((3, 4)),
-            dma((2,)), dma((9,)), dma((4,)), dma((4,)), dma((11,)), dma((11,)),
+            dma((2,)), dma((13,)), dma((2,)), dma((9,)), dma((4,)), dma((4,)), dma((11,)), dma((11,)),
         ]
     )
     vm = pl.BlockSpec(memory_space=pltpu.VMEM)

time: 132 us -> 125 us (0.947)
  Pallas kernels: 130 us -> 123 us
    pallas_call x1, Pallas kernels: 130 us -> 123 us  [layer(): pl.pallas_call(layer_kernel, out_shape=jax.ShapeDtypeStruct(tokens.shape,...]
where the time goes in v6:
time: 125 us
  Pallas kernels  123 us (98%)
  local copies, waits for them, and re-layouts  1.54 us (1%)
    pallas_call x1, Pallas kernels, layer(): pl.pallas_call(layer_kernel, out_shape=jax.ShapeDtypeStruct(tokens.shape,...  123 us

profile of v6, /device:TPU:1, one launch (start us, length us, event | category | flops | bytes accessed | tf_op | source)
XLA Modules:
  0.0 125.0 jit_solution(3159424842062945228)
XLA Ops:
  0.0 123.4 %layer.1 = bf16[16,2880]{1,0:T(8,128)(2,1)} custom-call(bf16[16,2880]{1,0:T(8,128)(2,1)} %tokens.1, f32[2880]{0:T(1024)} %attn_gain.1, f32[2880]{0:T(1024)} %mlp_gain.1, f32[4]{0:T(128)} %sinks.1, s32[4,16]{1,0:T(4,128)} %bitcast.10, s32[4,16]{1,0:T(4,128)} %bitcast.11, bf16[2880,256]{1,0:T(8,128)(2,1)} %query_hbm.1, bf16[64,2880]{1,0:T(8,128)(2,1)} %keyval_hbm.1, ...), custom_call_target="tpu_custom_call" | custom-call | tf_op jit(solution)/shard_map/layer/pallas_call | solution.py:755
  123.4 1.5 %copy.14 = bf16[16,2880]{1,0:T(8,128)(2,1)} copy(bf16[16,2880]{1,0:T(8,128)(2,1)} %layer.1) | data formatting | bytes 184320

commit v7 on v6

--- a/solution.py
+++ b/solution.py
@@ -472,41 +472,45 @@
         ag_wait(p, k + 3, mine(p, (ALL, j, 2), 1))
         forward(p, (ALL, j, 2))
 
+    def spread(p, by):
+        v = mine(p, (by, 0, 0))
+        for s, k in ((1, 3), (2, 9)):
+            up, dn = ways(p, s)
+            ag(p, k, v, up)
+            ag(p, k + 1, v, dn)
+
     for p in range(3):
         own = mine(p, (0, 0, 0))
         up, dn = ways(p, 0)
+        ag(p, 2, own, neighbour(ORDERS[p][0], 2))
         ag(p, 0, own, up)
         ag(p, 1, own, dn)
-        ag(p, 2, own, neighbour(ORDERS[p][0], 2))
+    for p in range(3):
+        spread(p, 0)
     for p in range(3):
         ag_wait(p, 0, mine(p, (-1, 0, 0)))
+        spread(p, -1)
         ag_wait(p, 1, mine(p, (1, 0, 0)))
+        spread(p, 1)
+    for p in range(3):
         ag_wait(p, 2, mine(p, (2, 0, 0)))
+        spread(p, 2)
+        forward(p, (ALL, 0, 0))
+    for p in range(3):
         up, dn = ways(p, 1)
-        ag(p, 3, mine(p, (ALL, 0, 0), 0), up)
-        ag(p, 4, mine(p, (ALL, 0, 0), 1), dn)
-        ag(p, 5, mine(p, (ALL, 0, 0), 1), up)
-        ag(p, 6, mine(p, (ALL, 0, 0), 0), dn)
-        third(p, 0)
-        forward(p, (ALL, 0, 0))
-    for p in range(3):
-        up, dn = ways(p, 1)
-        ag_wait(p, 3, mine(p, (ALL, -1, 0), 0))
-        ag(p, 7, mine(p, (ALL, -1, 0), 0), up)
-        ag_wait(p, 4, mine(p, (ALL, 1, 0), 1))
-        ag(p, 8, mine(p, (ALL, 1, 0), 1), dn)
-    for p in range(3):
-        ag_wait(p, 5, mine(p, (ALL, -1, 0), 1))
+        ag_wait(p, 3, mine(p, (ALL, -1, 0)))
+        ag(p, 5, mine(p, (ALL, -1, 0), 0), up)
         third(p, -1)
-        ag_wait(p, 6, mine(p, (ALL, 1, 0), 0))
+        ag_wait(p, 4, mine(p, (ALL, 1, 0)))
+        ag(p, 6, mine(p, (ALL, 1, 0), 1), dn)
         third(p, 1)
         forward(p, (ALL, -1, 0))
         forward(p, (ALL, 1, 0))
     for p in range(3):
         third_relay(p, 0)
     for p in range(3):
-        ag_wait(p, 7, mine(p, (ALL, 2, 0), 0))
-        ag_wait(p, 8, mine(p, (ALL, 2, 0), 1))
+        ag_wait(p, 5, mine(p, (ALL, 2, 0), 0))
+        ag_wait(p, 6, mine(p, (ALL, 2, 0), 1))
         third(p, 2)
         forward(p, (ALL, 2, 0))
     for p in range(3):

time: 125 us -> 124 us (level)
    pallas_call x1, Pallas kernels: 123 us -> 122 us  [layer(): pl.pallas_call(layer_kernel, out_shape=jax.ShapeDtypeStruct(tokens.shape,...]
where the time goes in v7:
time: 124 us
  Pallas kernels  122 us (98%)
  local copies, waits for them, and re-layouts  1.54 us (1%)
    pallas_call x1, Pallas kernels, layer(): pl.pallas_call(layer_kernel, out_shape=jax.ShapeDtypeStruct(tokens.shape,...  122 us

profile of v7, /device:TPU:1, one launch (start us, length us, event | category | flops | bytes accessed | tf_op | source)
XLA Modules:
  0.0 123.6 jit_solution(12815273613336501181)
XLA Ops:
  0.0 122.1 %layer.1 = bf16[16,2880]{1,0:T(8,128)(2,1)} custom-call(bf16[16,2880]{1,0:T(8,128)(2,1)} %tokens.1, f32[2880]{0:T(1024)} %attn_gain.1, f32[2880]{0:T(1024)} %mlp_gain.1, f32[4]{0:T(128)} %sinks.1, s32[4,16]{1,0:T(4,128)} %bitcast.10, s32[4,16]{1,0:T(4,128)} %bitcast.11, bf16[2880,256]{1,0:T(8,128)(2,1)} %query_hbm.1, bf16[64,2880]{1,0:T(8,128)(2,1)} %keyval_hbm.1, ...), custom_call_target="tpu_custom_call" | custom-call | tf_op jit(solution)/shard_map/layer/pallas_call | solution.py:759
  122.1 1.5 %copy.14 = bf16[16,2880]{1,0:T(8,128)(2,1)} copy(bf16[16,2880]{1,0:T(8,128)(2,1)} %layer.1) | data formatting | bytes 184320
